TPU v7x, 32 devices: a whole 2x2x4 slice. The times are simulated.
32 devices in a mesh: region: 2 (over y), cell: 16 (over z, x, core).
Axes of the slice: x: 2, y: 2, z: 4, core: 2. Of those that a mesh axis runs over, the one named last changes fastest.
Arguments:
- position: float32 [3, 256, 128], P(None, ('region', 'cell')), may hold values from 0 to 1
- velocity: float32 [3, 256, 128], P(None, ('region', 'cell')), may hold values from -6 to 6
- smoothing: float32 [256, 128], P(('region', 'cell')), may hold values from 0.3 to 0.5
- particle_mass: float32 [256, 128], P(('region', 'cell')), may hold values from 0.004 to 0.012
- energy: float32 [256, 128], P(('region', 'cell')), may hold values from 0.5 to 2
- density_old: float32 [256, 128], P(('region', 'cell')), may hold values from 0.3 to 1.2
- cell_count: int32 [256], P(('region', 'cell')), may hold values from 8 to 128, as said below
- active: int32 [256, 128], P(('region', 'cell')), may hold values from 0 to 1, as said below
- time_bin: int32 [256, 128], P(('region', 'cell')), may hold values from 0 to 5
- pair_source: int32 [256, 27], P(('region', 'cell')), may hold values from 0 to 41, as said below
- pair_shift: int32 [256, 27], P(('region', 'cell')), may hold values from 0 to 26, as said below
- export: int32 [512, 2], P(('region', 'cell')), may hold values from 0 to 7
Outputs:
- density: float32 [256, 128], P(('region', 'cell'))
- acceleration: float32 [3, 256, 128], P(None, ('region', 'cell'))
- kicked_velocity: float32 [3, 256, 128], P(None, ('region', 'cell'))
Inputs may be any that keep to these rules, and one draw needn't show every extreme that they name: `cell_count`: every device has a cell of exactly 128 particles. `active`: 0 in the slots past a cell's count. `pair_source`: pair 0 of a device's cell k names source k; a device's pairs name every one of its 42 sources. `pair_shift`: pair 0 has code 13; a cell's 27 codes are distinct.
All inputs are finite; a program needn't handle non-finite values.
Results may differ from a plain program's by a relative error of at most 0.0003.
Values sent between devices are 32-bit elements; how exact they have to be, the bound alone decides.
No kernel may reach another device: no remote copies, remote signals or barrier semaphores. Data moves between devices by JAX's collectives and lax.ppermute only.
A program may use at most 64 MiB of HBM per device.

v0:
```python
import functools
import math

import jax
import jax.numpy as jnp
from jax import lax
from jax.experimental import pallas as pl
from jax.experimental.pallas import tpu as pltpu
from jax.sharding import PartitionSpec as P

ADIABATIC = 5.0 / 3.0
STEP_MAX = 0.2
LANES = 128
ROWS = 8
FORCE_UNROLL = 7
PAIR_ROWS = 32
FAR_AWAY = 1e9
SPARE = FORCE_UNROLL

X, Y, Z, MASS, VX, VY, VZ, WIDE = range(ROWS)
HEAT, DENS, LIVE = range(3)
SENT = 4
INV6, HALF, SOUND, WARM, SUPPORT = range(5)


def lane_gather(values, index):
    return jnp.take_along_axis(values, index, axis=1, mode="promise_in_bounds")


def lanes_of(shape):
    return lax.broadcasted_iota(jnp.int32, shape, len(shape) - 1)


def start_copies(arrays, landed, sem):
    copies = [
        pltpu.make_async_copy(array, place, sem.at[index])
        for index, (array, place) in enumerate(zip(arrays, landed))
    ]
    for copy in copies:
        copy.start()
    return copies


def pack_kernel(count, *refs):
    arrays, (own, own_sent, outgoing, border) = refs[:7], refs[7:11]
    landed, sem = refs[11:-1], refs[-1]
    for copy in start_copies(arrays, landed, sem):
        copy.wait()
    export, position, velocity, smoothing, mass, energy, density_old = landed
    cells = smoothing.shape[0]
    shape = smoothing.shape
    lane = lanes_of(shape)
    row = lax.broadcasted_iota(jnp.int32, shape, 0)
    counts = jnp.zeros(shape, jnp.int32)
    for cell in range(cells):
        counts = jnp.where(row == cell, count[cell], counts)
    mass_live = jnp.where(lane < counts, mass[...], 0.0)
    rows = (
        position[0], position[1], position[2], mass_live,
        40.0 * velocity[0], 40.0 * velocity[1], 40.0 * velocity[2], 2.0 * smoothing[...],
    )
    for field, values in enumerate(rows):
        own[:, field, :] = values
    own_sent[:, HEAT, :] = (ADIABATIC - 1.0) * energy[...]
    own_sent[:, DENS, :] = density_old[...]
    own_sent[:, LIVE, :] = counts.astype(jnp.float32)
    own_sent[:, SENT - 1, :] = jnp.zeros(shape, jnp.float32)
    per_peer, peers = export.shape
    for peer in range(peers):
        for entry in range(per_peer):
            cell = export[entry, peer]
            outgoing[peer, entry * ROWS : (entry + 1) * ROWS, :] = own[cell]
            start = per_peer * ROWS + entry * SENT
            outgoing[peer, start : start + SENT, :] = own_sent[cell]
    for side, cell in enumerate((cells - 1, 0)):
        border[side, 0:ROWS, :] = own[cell]
        border[side, ROWS : ROWS + SENT, :] = own_sent[cell]


def sort_kernel(*refs):
    rank_out, actives, columns, heat_sorted, wide_sorted, lowest, highest, reach = refs[3:11]
    landed, sem = refs[11:14], refs[14]
    for copy in start_copies(refs[:3], landed, sem):
        copy.wait()
    own, own_sent, active = landed
    shape = active.shape
    cells = shape[0]
    lane = lanes_of(shape)
    is_active = active[...] > 0
    ones = jnp.where(is_active, 1.0, 0.0)
    for cell in range(cells):
        actives[0, cell] = jnp.sum(ones[cell : cell + 1, :]).astype(jnp.int32)
    square = (LANES, LANES)
    upper = lax.broadcasted_iota(jnp.int32, square, 0) <= lanes_of(square)
    upper = jnp.where(upper, 1.0, 0.0).astype(jnp.bfloat16)
    seen = jnp.dot(ones.astype(jnp.bfloat16), upper, preferred_element_type=jnp.float32)
    seen = seen.astype(jnp.int32)
    chosen = lane_gather(seen, jnp.full(shape, LANES - 1, jnp.int32))
    others = lane + 1 - seen
    rank_out[...] = jnp.where(is_active, seen - 1, chosen + others - 1)
    first_part = lane < chosen
    wanted = jnp.where(first_part, lane, lane - chosen)
    slot = jnp.zeros(shape, jnp.int32)
    step = LANES // 2
    while step:
        probe = slot + (step - 1)
        found = jnp.where(first_part, lane_gather(seen, probe), lane_gather(others, probe))
        slot = jnp.where(found <= wanted, slot + step, slot)
        step //= 2
    for cell in range(cells):
        order = jnp.broadcast_to(slot[cell : cell + 1, :], (ROWS, LANES))
        tile = lane_gather(own[cell], order)
        columns[cell] = tile.T
        target = lane < chosen[cell : cell + 1, :]
        low = jnp.min(jnp.where(target, tile, FAR_AWAY), axis=1, keepdims=True)
        high = jnp.max(jnp.where(target, tile, -FAR_AWAY), axis=1, keepdims=True)
        place = lax.broadcasted_iota(jnp.int32, shape, 0) <= Z
        lowest[cell] = jnp.where(place, low, -FAR_AWAY)
        highest[cell] = jnp.where(place, high, FAR_AWAY)
        reach[cell : cell + 1, :] = jnp.broadcast_to(high[WIDE : WIDE + 1, :], (1, LANES))
        wide_sorted[cell : cell + 1, :] = tile[WIDE : WIDE + 1, :]
        warm = jnp.broadcast_to(own_sent[cell, HEAT : HEAT + 1, :], (ROWS, LANES))
        heat_sorted[cell : cell + 1, :] = lane_gather(warm, order)[0:1, :]


def source_tiles(own, incoming, border, per_peer):
    cells, peers = own[0].shape[0], incoming.shape[0]
    for cell in range(cells):
        yield cell, lambda c=cell: own[0][c], lambda c=cell: own[1][c]
    for peer in range(peers):
        for entry in range(per_peer):
            near, sent = entry * ROWS, per_peer * ROWS + entry * SENT
            yield (
                cells + peer * per_peer + entry,
                lambda p=peer, n=near: incoming[p, n : n + ROWS, :],
                lambda p=peer, n=sent: incoming[p, n : n + SENT, :],
            )
    for side in range(2):
        yield (
            cells + peers * per_peer + side,
            lambda b=side: border[b, 0:ROWS, :],
            lambda b=side: border[b, ROWS : ROWS + SENT, :],
        )


def fill_shifts(shifts):
    row = lax.broadcasted_iota(jnp.int32, (ROWS, LANES), 0)
    for code in range(shifts.shape[0]):
        first, second, third = code // 9 - 1.0, code // 3 % 3 - 1.0, code % 3 - 1.0
        shifts[code] = jnp.where(
            row == X, first, jnp.where(row == Y, second, jnp.where(row == Z, third, 0.0))
        )


def fill_streams(streams, tables, sources, starts, orders, cell):
    shape = (ROWS, LANES)
    lane = lanes_of(shape)
    pairs = sources.shape[1]
    moved = []
    for pair in range(pairs):
        order = jnp.broadcast_to(orders(pair), shape)
        moved.append([lane_gather(load(sources[cell, pair], pair), order) for load in tables])
    for pair in range(pairs):
        start = starts(pair)
        block = start >> 7
        fresh = lane >= (start & (LANES - 1))
        for which, stream in enumerate(streams):
            stream[block + 1] = moved[pair][which]
            pltpu.store(stream.at[block], moved[pair][which], mask=fresh)
    end = starts(pairs)
    block = end >> 7
    for stream in streams:
        stream[block] = jnp.where(lane < (end & (LANES - 1)), stream[block], 0.0)
        for extra in range(1, SPARE):
            stream[block + extra] = jnp.zeros(shape, jnp.float32)
    return (end + LANES - 1) >> 7


def spread(values, field):
    return jnp.broadcast_to(values[:, field : field + 1], (values.shape[0], LANES))


def over_targets(active, one_chunk):
    groups = (active + ROWS - 1) // ROWS

    def large(chunk, carry):
        one_chunk(pl.multiple_of(chunk * 4 * ROWS, ROWS), 4)
        return carry

    lax.fori_loop(0, groups // 4, large, 0)
    for size in (2, 1):

        @pl.when((groups & size) != 0)
        def _(size=size):
            done = groups & -(2 * size)
            one_chunk(pl.multiple_of(done * ROWS, ROWS), size)


def density_kernel(per_peer, *refs):
    arrays, (density, sorted_density, outgoing, outgoing_border) = refs[:13], refs[13:17]
    landed, (sem, table, shifts, sums, lines) = refs[17:30], refs[30:]
    copies = start_copies(arrays, landed, sem)
    fill_shifts(shifts)
    for copy in copies:
        copy.wait()
    pair_source, pair_shift, export, actives = landed[:4]
    own, own_sent, incoming, border, rank, columns, wide_sorted, active, density_old = landed[4:]
    cells, peers = own.shape[0], incoming.shape[0]
    for place, near, _ in source_tiles((own, own_sent), incoming, border, per_peer):
        table[place] = near()

    def one_cell(cell, carry):
        def one_chunk(base, groups):
            size = groups * ROWS
            mine = columns[cell, pl.ds(base, size), :]
            place = [spread(mine, field) for field in (X, Y, Z)]
            wide = spread(mine, WIDE)
            smooth = 0.5 * wide

            total = jnp.zeros((size, LANES), jnp.float32)
            for pair in range(pair_source.shape[1]):
                source, code = pair_source[cell, pair], pair_shift[cell, pair]
                s = lambda field: table[source, field : field + 1, :]
                shift = lambda field: shifts[code, field : field + 1, :]
                apart = [place[c] - (s(c) + shift(c)) for c in range(3)]
                square = apart[0] * apart[0] + apart[1] * apart[1] + apart[2] * apart[2]
                radius = square * lax.rsqrt(jnp.maximum(square, 1e-24))
                outer = jnp.maximum(wide - radius, 0.0)
                inner = jnp.maximum(smooth - radius, 0.0)
                value = outer * outer * outer - 4.0 * (inner * inner * inner)
                total = total + s(MASS) * value
            sums[cell, pl.ds(base, size), 0:1] = jnp.sum(total, axis=1, keepdims=True)

        over_targets(actives[0, cell], one_chunk)
        return carry

    lax.fori_loop(0, cells, one_cell, 0)
    for cell in range(cells):
        lines[cell : cell + 1, :] = sums[cell].T[0:1, :]
    inverse = 2.0 / wide_sorted[...]
    inverse = inverse * inverse * inverse
    summed = lines[...] * (0.25 / math.pi) * (inverse * inverse)
    sorted_density[...] = summed
    density[...] = jnp.where(active[...] > 0, lane_gather(summed, rank[...]), density_old[...])
    for peer in range(peers):
        for entry in range(per_peer):
            outgoing[peer, entry : entry + 1, :] = density[pl.ds(export[entry, peer], 1), :]
    outgoing_border[0:1, :] = density[cells - 1 : cells, :]
    outgoing_border[1:2, :] = density[0:1, :]


def stream_kernel(per_peer, *refs):
    arrays, (near_out, far_out, starts, orders, more) = refs[:12], refs[12:17]
    landed, refs = refs[17:29], refs[29:]
    sems, near_table, far_table, shifts, inside, totals_row, totals, sem = refs[:8]
    near_streams, far_streams, out_sems = refs[8:]
    copies = start_copies(arrays, landed, sems)
    fill_shifts(shifts)
    for copy in copies:
        copy.wait()
    pair_source, pair_shift, own, own_sent, incoming, border = landed[:6]
    wide_sorted, heat_sorted, sorted_density, lowest, highest, reach = landed[6:]
    cells, pairs = pair_source.shape
    tile_shape = (ROWS, LANES)
    row = lax.broadcasted_iota(jnp.int32, tile_shape, 0)
    lane = lanes_of(tile_shape).astype(jnp.float32)
    for place, near, sent in source_tiles((own, own_sent), incoming, border, per_peer):
        tile, other = near(), sent()
        near_table[place] = tile
        wide, heat = tile[WIDE : WIDE + 1, :], other[HEAT : HEAT + 1, :]
        inverse = 2.0 * pl.reciprocal(wide, approx=True)
        inverse = inverse * inverse * inverse
        far_table[place, INV6 : INV6 + 1, :] = inverse * inverse
        far_table[place, HALF : HALF + 1, :] = 0.025 * wide
        far_table[place, SOUND : SOUND + 1, :] = jnp.sqrt(ADIABATIC * heat)
        far_table[place, WARM : WARM + 1, :] = heat
        far_table[place, SUPPORT : SUPPORT + 1, :] = jnp.where(
            lane[0:1, :] < other[LIVE : LIVE + 1, :], wide, -FAR_AWAY
        )

    def choose(cell, carry):
        low, high = lowest[cell], highest[cell]
        widest = reach[pl.ds(cell, 1), :]
        kept = []
        for pair in range(pairs):
            source = pair_source[cell, pair]
            tile = near_table[source] + shifts[pair_shift[cell, pair]]
            away = jnp.maximum(jnp.maximum(low - tile, tile - high), 0.0)
            distance = jnp.sum(away * away, axis=0, keepdims=True)
            support = far_table[source, SUPPORT : SUPPORT + 1, :]
            limit = jnp.maximum(support, widest)
            keep = (distance < limit * limit) & (support > 0.0)
            kept.append(jnp.where(keep, 1.0, 0.0))
        kept += [jnp.zeros((1, LANES), jnp.float32)] * (PAIR_ROWS - pairs)
        base = pl.multiple_of(cell * PAIR_ROWS, PAIR_ROWS)
        inside[pl.ds(base, PAIR_ROWS), :] = jnp.concatenate(kept, axis=0)
        return carry

    lax.fori_loop(0, cells, choose, 0)
    flags = inside[...].astype(jnp.bfloat16)
    all_lanes = jnp.ones((ROWS, LANES), jnp.bfloat16)
    sums = lax.dot_general(
        all_lanes, flags, (((1,), (1,)), ((), ())), preferred_element_type=jnp.float32
    )
    for line in range(totals_row.shape[0]):
        totals_row[line : line + 1, :] = sums[0:1, line * LANES : (line + 1) * LANES].astype(
            jnp.int32
        )
    copy = pltpu.make_async_copy(totals_row, totals, sem)
    copy.start()
    square = (LANES, LANES)
    upper = lax.broadcasted_iota(jnp.int32, square, 0) <= lanes_of(square)
    upper = jnp.where(upper, 1.0, 0.0).astype(jnp.bfloat16)
    seen = jnp.dot(flags, upper, preferred_element_type=jnp.float32)
    wanted = lanes_of(seen.shape).astype(jnp.float32)
    slot = jnp.zeros(seen.shape, jnp.int32)
    step = LANES // 2
    while step:
        found = lane_gather(seen, slot + (step - 1))
        slot = jnp.where(found <= wanted, slot + step, slot)
        step //= 2
    orders[...] = slot
    inverse = 2.0 * pl.reciprocal(wide_sorted[...], approx=True)
    inverse = inverse * inverse * inverse
    fields = (
        inverse * inverse, 0.025 * wide_sorted[...], jnp.sqrt(ADIABATIC * heat_sorted[...]),
        4.0 * sorted_density[...], heat_sorted[...] / sorted_density[...],
    )
    for cell in range(cells):
        tile = jnp.zeros(tile_shape, jnp.float32)
        for which, values in enumerate(fields):
            tile = jnp.where(row == which, values[cell : cell + 1, :], tile)
        more[cell] = tile.T
    copy.wait()

    def leave(cell):
        return [
            pltpu.make_async_copy(stream.at[cell], out.at[cell], sems.at[cell])
            for stream, out, sems in (
                (near_streams, near_out, out_sems.at[0]), (far_streams, far_out, out_sems.at[1]),
            )
        ]

    def one_cell(cell, carry):
        tables = (
            lambda source, pair: near_table[source] + shifts[pair_shift[cell, pair]],
            lambda source, pair: far_table[source],
        )
        start = jnp.int32(0)
        begins, turned = [], []
        for pair in range(pairs):
            begins.append(start)
            place = cell * PAIR_ROWS + pair
            turned.append(pltpu.roll(orders[pl.ds(place, 1), :], start & (LANES - 1), 1))
            start = start + totals[place >> 7, place & (LANES - 1)]
        begins.append(start)
        turned += [turned[-1]] * (PAIR_ROWS - pairs)
        for pair, begin in enumerate(begins):
            starts[cell, pair] = begin
        fill_streams(
            (near_streams.at[cell], far_streams.at[cell]), tables, pair_source,
            lambda pair: begins[pair], lambda pair: turned[pair], cell,
        )
        base = pl.multiple_of(cell * PAIR_ROWS, PAIR_ROWS)
        orders[pl.ds(base, PAIR_ROWS), :] = jnp.concatenate(turned, axis=0)
        for copy in leave(cell):
            copy.start()
        return carry

    lax.fori_loop(0, cells, one_cell, 0)
    for cell in range(cells):
        for copy in leave(cell):
            copy.wait()


def force_kernel(per_peer, *refs):
    arrays, streams, (acceleration, kicked) = refs[:13], refs[13:15], refs[15:17]
    landed, sem, landed_streams, stream_sems = refs[17:30], refs[30], refs[31:33], refs[33:35]
    table, stream, sums, lines = refs[35:]
    copies = start_copies(arrays, landed, sem)

    def stream_copies(cell):
        return [
            pltpu.make_async_copy(source.at[cell], place.at[cell], sems.at[cell])
            for source, place, sems in zip(streams, landed_streams, stream_sems)
        ]

    for cell in range(streams[0].shape[0]):
        for copy in stream_copies(cell):
            copy.start()
    for copy in copies:
        copy.wait()
    pair_source, starts, actives, columns, more, orders, own_density = landed[:7]
    new_density, new_border, rank, active, velocity, time_bin = landed[7:]
    near_streams, far_streams = landed_streams
    cells, peers = own_density.shape[0], new_density.shape[0]
    for cell in range(cells):
        table[cell, 0:1, :] = own_density[cell : cell + 1, :]
    for peer in range(peers):
        for entry in range(per_peer):
            place = cells + peer * per_peer + entry
            table[place, 0:1, :] = new_density[peer, entry : entry + 1, :]
    for side in range(2):
        table[cells + peers * per_peer + side, 0:1, :] = new_border[side : side + 1, :]

    def one_cell(cell, carry):
        near, far = near_streams.at[cell], far_streams.at[cell]
        used = fill_streams(
            (stream,), (lambda source, pair: table[source],), pair_source,
            lambda pair: starts[cell, pair],
            lambda pair: orders[pl.ds(cell * PAIR_ROWS + pair, 1), :], cell,
        )
        for copy in stream_copies(cell):
            copy.wait()
        rounds = (used + FORCE_UNROLL - 1) // FORCE_UNROLL

        def one_chunk(base, groups):
            size = groups * ROWS
            mine = columns[cell, pl.ds(base, size), :]
            mine_more = more[cell, pl.ds(base, size), :]
            place = [spread(mine, field) for field in (X, Y, Z)]
            speed = [spread(mine, field) for field in (VX, VY, VZ)]
            wide = spread(mine, WIDE)
            inv6, half_, sound, dens4, press = [spread(mine_more, field) for field in range(5)]

            def blocks(index, totals):
                for sub in range(FORCE_UNROLL):
                    block = index * FORCE_UNROLL + sub
                    s = lambda field: near[block, field : field + 1, :]
                    o = lambda field: far[block, field : field + 1, :]
                    dens = stream[block, 0:1, :]
                    their_press = o(WARM) * pl.reciprocal(jnp.maximum(dens, 1e-30), approx=True)
                    apart = [place[c] - s(c) for c in range(3)]
                    square = apart[0] * apart[0] + apart[1] * apart[1] + apart[2] * apart[2]
                    inverse = lax.rsqrt(jnp.maximum(square, 1e-24))
                    radius = square * inverse
                    double = radius + radius
                    outer = jnp.maximum(wide - radius, 0.0)
                    inner = jnp.maximum(wide - double, 0.0)
                    slope = inv6 * (outer * outer - inner * inner)
                    outer = jnp.maximum(s(WIDE) - radius, 0.0)
                    inner = jnp.maximum(s(WIDE) - double, 0.0)
                    slope = slope + o(INV6) * (outer * outer - inner * inner)
                    approach = (
                        (speed[0] - s(VX)) * apart[0]
                        + (speed[1] - s(VY)) * apart[1]
                        + (speed[2] - s(VZ)) * apart[2]
                    )
                    half = half_ + o(HALF)
                    slow = pl.reciprocal(square + half * half, approx=True)
                    mu = half * jnp.minimum(approach, 0.0) * slow
                    light = pl.reciprocal(dens4 + 4.0 * dens, approx=True)
                    viscous = mu * (mu - (sound + o(SOUND))) * light
                    weight = (press + their_press + viscous) * (slope * (inverse * s(MASS)))
                    totals = tuple(total + weight * a for total, a in zip(totals, apart))
                return totals

            zero = jnp.zeros((size, LANES), jnp.float32)
            totals = lax.fori_loop(0, rounds, blocks, (zero, zero, zero))
            for c in range(3):
                sums[cell, pl.ds(base, size), c : c + 1] = jnp.sum(
                    totals[c], axis=1, keepdims=True
                )

        over_targets(actives[0, cell], one_chunk)
        return carry

    lax.fori_loop(0, cells, one_cell, 0)
    for cell in range(cells):
        turned = sums[cell].T
        for c in range(3):
            lines[c, cell : cell + 1, :] = turned[c : c + 1, :]
    step = STEP_MAX * jnp.exp2(-time_bin[...].astype(jnp.float32))
    for c in range(3):
        gathered = lane_gather(lines[c] * (0.375 / math.pi), rank[...])
        value = jnp.where(active[...] > 0, gathered, 0.0)
        acceleration[c] = value
        kicked[c] = velocity[c] + value * step


def shards(
    position, velocity, smoothing, particle_mass, energy, density_old, cell_count, active,
    time_bin, pair_source, pair_shift, export,
):
    cells, capacity = smoothing.shape
    peers, per_peer = export.shape
    sources = cells + peers * per_peer + 2
    codes = 27
    f32 = lambda *shape: jax.ShapeDtypeStruct(shape, jnp.float32)
    smem = pl.BlockSpec(memory_space=pltpu.SMEM)
    vmem = pl.BlockSpec(memory_space=pltpu.VMEM)
    hbm = pl.BlockSpec(memory_space=pltpu.HBM)
    whole = pltpu.CompilerParams(vmem_limit_bytes=64 * 2**20)
    i32 = lambda *shape: jax.ShapeDtypeStruct(shape, jnp.int32)
    sent_rows = per_peer * (ROWS + SENT)
    turned = export.T

    def landing(scalars, *arrays):
        return (
            [pltpu.SMEM(a.shape, a.dtype) for a in arrays[:scalars]]
            + [pltpu.VMEM(a.shape, a.dtype) for a in arrays[scalars:]]
            + [pltpu.SemaphoreType.DMA((len(arrays),))]
        )

    arrays = (turned, position, velocity, smoothing, particle_mass, energy, density_old)
    own, own_sent, outgoing, border = pl.pallas_call(
        pack_kernel,
        out_shape=(
            f32(cells, ROWS, capacity),
            f32(cells, SENT, capacity),
            f32(peers, sent_rows, capacity),
            f32(2, ROWS + SENT, capacity),
        ),
        in_specs=[smem] + [hbm] * 7,
        out_specs=(vmem,) * 4,
        scratch_shapes=landing(1, *arrays),
        compiler_params=whole,
        name="pack",
    )(cell_count, *arrays)

    def exchange(pieces):
        return lax.all_to_all(pieces, "cell", split_axis=0, concat_axis=0, tiled=True)

    def swap_border(pieces):
        size = lax.axis_size("region")
        up = [(i, (i + 1) % size) for i in range(size)]
        down = [(j, i) for i, j in up]
        if size == 2:
            return lax.ppermute(pieces, "region", up)
        before = lax.ppermute(pieces[0:1], "region", up)
        after = lax.ppermute(pieces[1:2], "region", down)
        return jnp.concatenate([before, after], axis=0)

    incoming = exchange(outgoing)
    other = swap_border(border)
    rank, actives, columns, heat_sorted, wide_sorted, lowest, highest, reach = pl.pallas_call(
        sort_kernel,
        out_shape=(
            i32(cells, capacity),
            i32(1, cells),
            f32(cells, capacity, ROWS),
            f32(cells, capacity),
            f32(cells, capacity),
            f32(cells, ROWS, capacity),
            f32(cells, ROWS, capacity),
            f32(cells, capacity),
        ),
        in_specs=[hbm] * 3,
        out_specs=(vmem, smem) + (vmem,) * 6,
        scratch_shapes=landing(0, own, own_sent, active),
        compiler_params=whole,
        name="sort",
    )(own, own_sent, active)

    arrays = (
        pair_source, pair_shift, turned, actives,
        own, own_sent, incoming, other, rank, columns, wide_sorted, active, density_old,
    )
    density, sorted_density, outgoing_density, border_density = pl.pallas_call(
        functools.partial(density_kernel, per_peer),
        out_shape=(
            f32(cells, capacity),
            f32(cells, capacity),
            f32(peers, per_peer, capacity),
            f32(2, capacity),
        ),
        in_specs=[hbm] * 13,
        out_specs=(vmem,) * 4,
        scratch_shapes=landing(4, *arrays)
        + [
            pltpu.VMEM((sources, ROWS, capacity), jnp.float32),
            pltpu.VMEM((codes, ROWS, capacity), jnp.float32),
            pltpu.VMEM((cells, capacity, ROWS), jnp.float32),
            pltpu.VMEM((cells, capacity), jnp.float32),
        ],
        compiler_params=whole,
        name="density",
    )(*arrays)

    new_density = exchange(outgoing_density)
    new_border = swap_border(border_density)
    pairs = pair_source.shape[1]
    blocks = pairs + SPARE
    pair_rows = cells * PAIR_ROWS
    arrays = (
        pair_source, pair_shift, own, own_sent, incoming, other, wide_sorted, heat_sorted,
        sorted_density, lowest, highest, reach,
    )
    near_streams, far_streams, starts, orders, more = pl.pallas_call(
        functools.partial(stream_kernel, per_peer),
        out_shape=(
            f32(cells, blocks, ROWS, capacity),
            f32(cells, blocks, ROWS, capacity),
            i32(cells, pairs + 1),
            i32(pair_rows, capacity),
            f32(cells, capacity, ROWS),
        ),
        in_specs=[hbm] * 12,
        out_specs=(hbm, hbm, smem, vmem, vmem),
        scratch_shapes=landing(2, *arrays)
        + [
            pltpu.VMEM((sources, ROWS, capacity), jnp.float32),
            pltpu.VMEM((sources, ROWS, capacity), jnp.float32),
            pltpu.VMEM((codes, ROWS, capacity), jnp.float32),
            pltpu.VMEM((pair_rows, capacity), jnp.float32),
            pltpu.VMEM((pair_rows // capacity, capacity), jnp.int32),
            pltpu.SMEM((pair_rows // capacity, capacity), jnp.int32),
            pltpu.SemaphoreType.DMA,
            pltpu.VMEM((cells, blocks, ROWS, capacity), jnp.float32),
            pltpu.VMEM((cells, blocks, ROWS, capacity), jnp.float32),
            pltpu.SemaphoreType.DMA((2, cells)),
        ],
        compiler_params=whole,
        name="streams",
    )(*arrays)

    arrays = (
        pair_source, starts, actives,
        columns, more, orders, density, new_density, new_border, rank, active, velocity, time_bin,
    )
    acceleration, kicked = pl.pallas_call(
        functools.partial(force_kernel, per_peer),
        out_shape=(f32(3, cells, capacity), f32(3, cells, capacity)),
        in_specs=[hbm] * 15,
        out_specs=(vmem,) * 2,
        scratch_shapes=landing(3, *arrays)
        + [pltpu.VMEM(near_streams.shape, jnp.float32)] * 2
        + [pltpu.SemaphoreType.DMA((cells,))] * 2
        + [
            pltpu.VMEM((sources, ROWS, capacity), jnp.float32),
            pltpu.VMEM((blocks, ROWS, capacity), jnp.float32),
            pltpu.VMEM((cells, capacity, ROWS), jnp.float32),
            pltpu.VMEM((3, cells, capacity), jnp.float32),
        ],
        compiler_params=whole,
        name="force",
    )(*arrays, near_streams, far_streams)
    return density, acceleration, kicked


def solution(mesh):
    rows = P(("region", "cell"), None)
    planes = P(None, ("region", "cell"), None)
    return jax.shard_map(
        shards,
        mesh=mesh,
        in_specs=(
            planes, planes, rows, rows, rows, rows, P(("region", "cell")), rows, rows, rows, rows,
            rows,
        ),
        out_specs=(rows, planes, planes),
        check_vma=False,
    )
```

profile of v0, /device:TPU:0, one launch (start us, length us, event | category | flops | bytes accessed | tf_op | source)
XLA Modules:
  0.0 48.9 jit_solution(12777503125716498618)
XLA Ops:
  0.6 2.3 %pack.1 = (f32[8,8,128]{2,1,0:T(8,128)}, f32[8,4,128]{2,1,0:T(4,128)}, f32[16,24,128]{2,1,0:T(8,128)}, f32[2,12,128]{2,1,0:T(8,128)}) custom-call(s32[8]{0:T(128)} %count.1, s32[2,16]{1,0:T(2,128)} %bitcast.1, f32[3,8,128]{2,1,0:T(8,128)} %refs_1_.3, f32[3,8,128]{2,1,0:T(8,128)} %refs_11_.3, f32[8,128]{1,0:T(8,128)} %refs_3_.1, f32[8,128]{1,0:T(8,128)} %refs_4_.1, ...), custom_call_target="tpu_custom_call" | custom-call | tf_op jit(solution)/shard_map/pack/pallas_call | solution.py:506
  2.9 7.4 %all-to-all-start = ((f32[16,24,128]{2,1,0:T(8,128)}), f32[16,24,128]{2,1,0:T(8,128)}, u32[]{:S(2)}, u32[]{:S(2)}) async-start(f32[16,24,128]{2,1,0:T(8,128)} %get-tuple-element.29), calls=%async_computation | async-start | bytes 393216 | tf_op jit(solution)/shard_map/all_to_all | solution.py:522
  10.4 1.6 %collective-permute-start = (f32[2,12,128]{2,1,0:T(8,128)}, f32[2,12,128]{2,1,0:T(8,128)}, u32[]{:S(2)}, u32[]{:S(2)}) collective-permute-start(f32[2,12,128]{2,1,0:T(8,128)} %get-tuple-element.30), channel_id=1, source_target_pairs={{0,16},{16,0},{1,17},{17,1},{2,18},{18,2},{3,19},{19,3},{4,20},{20... | collective-permute-start | bytes 36872 | tf_op jit(solution)/shard_map/ppermute | solution.py:529
  11.9 2.7 %sort.1 = (s32[8,128]{1,0:T(8,128)}, s32[1,8]{1,0:T(1,128)}, f32[8,128,8]{2,1,0:T(8,128)}, f32[8,128]{1,0:T(8,128)}, f32[8,128]{1,0:T(8,128)}, /*index=5*/f32[8,...) custom-call(f32[8,8,128]{2,1,0:T(8,128)} %get-tuple-element.26.refs_0_.refs_4_.refs_2_, ...), custom_call_target="tpu_custom_call" | custom-call | tf_op jit(solution)/shard_map/sort/pallas_call | solution.py:536
  14.6 0.0 collective-permute-done.refs_7_.refs_5_
  14.6 4.8 %all-to-all-done.refs_6_.refs_4_ = f32[16,24,128]{2,1,0:T(8,128)} async-done(((f32[16,24,128]{2,1,0:T(8,128)}), f32[16,24,128]{2,1,0:T(8,128)}, u32[]{:S(2)}, u32[]{:S(2)}) %all-to-all-start) | async-done | bytes 196640 | tf_op jit(solution)/shard_map/all_to_all | solution.py:522
  19.4 5.9 %density.1 = (f32[8,128]{1,0:T(8,128)}, f32[8,128]{1,0:T(8,128)}, f32[16,2,128]{2,1,0:T(2,128)}, f32[2,128]{1,0:T(2,128)}) custom-call(s32[8,27]{1,0:T(8,128)} %refs_0_.5, s32[8,27]{1,0:T(8,128)} %refs_1_.5, s32[2,16]{1,0:T(2,128)} %bitcast.2, s32[1,8]{1,0:T(1,128)} %get-tuple-element.28.refs_3_.refs_2_, ...), custom_call_target="tpu_custom_call" | custom-call | tf_op jit(solution)/shard_map/density/pallas_call | solution.py:559
  25.3 4.1 %all-to-all-start.1 = ((f32[16,2,128]{2,1,0:T(2,128)}), f32[16,2,128]{2,1,0:T(2,128)}, u32[]{:S(2)}, u32[]{:S(2)}) async-start(f32[16,2,128]{2,1,0:T(2,128)} %get-tuple-element.43), calls=%async_computation.1 | async-start | bytes 32768 | tf_op jit(solution)/shard_map/all_to_all | solution.py:522
  29.4 2.3 %collective-permute-start.1 = (f32[2,128]{1,0:T(2,128)}, f32[2,128]{1,0:T(2,128)}, u32[]{:S(2)}, u32[]{:S(2)}) collective-permute-start(f32[2,128]{1,0:T(2,128)} %get-tuple-element.44), channel_id=1, source_target_pairs={{0,16},{16,0},{1,17},{17,1},{2,18},{18,2},{3,19},{19,3},{4,20},{20... | collective-permute-start | bytes 3080 | tf_op jit(solution)/shard_map/ppermute | solution.py:529
  31.7 7.4 %streams.1 = (f32[8,34,8,128]{3,2,1,0:T(8,128)}, f32[8,34,8,128]{3,2,1,0:T(8,128)}, s32[8,28]{1,0:T(8,128)}, s32[256,128]{1,0:T(8,128)}, f32[8,128,8]{2,1,0:T(8,128)}) custom-call(s32[8,27]{1,0:T(8,128)} %refs_0_.5, s32[8,27]{1,0:T(8,128)} %refs_1_.5, f32[8,8,128]{2,1,0:T(8,128)} %get-tuple-element.26.refs_0_.refs_4_.refs_2_, ...), custom_call_target="tpu_custom_call" | custom-call | tf_op jit(solution)/shard_map/streams/pallas_call | solution.py:589
  39.1 0.0 collective-permute-done.1.refs_8_
  39.1 0.0 all-to-all-done.1.refs_7_
  39.1 9.8 %force.1 = (f32[3,8,128]{2,1,0:T(8,128)}, f32[3,8,128]{2,1,0:T(8,128)}) custom-call(s32[8,27]{1,0:T(8,128)} %refs_0_.5, s32[8,28]{1,0:T(8,128)} %get-tuple-element.40.refs_1_, s32[1,8]{1,0:T(1,128)} %get-tuple-element.28.refs_3_.refs_2_, f32[8,128,8]{2,1,0:T(8,128)} %get-tuple-element.32.refs_9_.refs_3_, f32[8,128,8]{2,1,0:T(8,128)} %get-tuple-element.41.refs_4_, ...), custom_call_target="tpu_custom_call" | custom-call | tf_op jit(solution)/shard_map/force/pallas_call | solution.py:621
Async XLA Ops:
  2.9 16.5 %all-to-all-start = ((f32[16,24,128]{2,1,0:T(8,128)}), f32[16,24,128]{2,1,0:T(8,128)}, u32[]{:S(2)}, u32[]{:S(2)}) async-start(f32[16,24,128]{2,1,0:T(8,128)} %get-tuple-element.29), calls=%async_computation | async-start | bytes 393216 | tf_op jit(solution)/shard_map/all_to_all | solution.py:522
  10.4 4.3 %collective-permute-start = (f32[2,12,128]{2,1,0:T(8,128)}, f32[2,12,128]{2,1,0:T(8,128)}, u32[]{:S(2)}, u32[]{:S(2)}) collective-permute-start(f32[2,12,128]{2,1,0:T(8,128)} %get-tuple-element.30), channel_id=1, source_target_pairs={{0,16},{16,0},{1,17},{17,1},{2,18},{18,2},{3,19},{19,3},{4,20},{20... | collective-permute-start | bytes 36872 | tf_op jit(solution)/shard_map/ppermute | solution.py:529
  25.3 13.8 %all-to-all-start.1 = ((f32[16,2,128]{2,1,0:T(2,128)}), f32[16,2,128]{2,1,0:T(2,128)}, u32[]{:S(2)}, u32[]{:S(2)}) async-start(f32[16,2,128]{2,1,0:T(2,128)} %get-tuple-element.43), calls=%async_computation.1 | async-start | bytes 32768 | tf_op jit(solution)/shard_map/all_to_all | solution.py:522
  29.4 9.7 %collective-permute-start.1 = (f32[2,128]{1,0:T(2,128)}, f32[2,128]{1,0:T(2,128)}, u32[]{:S(2)}, u32[]{:S(2)}) collective-permute-start(f32[2,128]{1,0:T(2,128)} %get-tuple-element.44), channel_id=1, source_target_pairs={{0,16},{16,0},{1,17},{17,1},{2,18},{18,2},{3,19},{19,3},{4,20},{20... | collective-permute-start | bytes 3080 | tf_op jit(solution)/shard_map/ppermute | solution.py:529
where the time goes:
time: 48.5 us; the launch traced here: 48.9 us
  Pallas kernels  28 us (58%)
  starting transfers between devices  15.4 us (32%)
  waiting for transfers between devices  4.78 us (10%)
  between operations  0.7 us (1%)
    all_to_all x2, starting transfers between devices, exchange(): lax.all_to_all(pieces, 'cell', split_axis=0, concat_axis=0, tiled=True)  11.5 us
    pallas_call x1, Pallas kernels, shards(): pl.pallas_call(functools.partial(force_kernel, per_peer), out_shape=(f32(...  9.8 us
    pallas_call x1, Pallas kernels, shards(): pl.pallas_call(functools.partial(stream_kernel, per_peer), out_shape=(f32...  7.38 us
    pallas_call x1, Pallas kernels, shards(): pl.pallas_call(functools.partial(density_kernel, per_peer), out_shape=(f3...  5.87 us
    all_to_all x2, waiting for transfers between devices, exchange(): lax.all_to_all(pieces, 'cell', split_axis=0, concat_axis=0, tiled=True)  4.77 us
    ppermute x2, starting transfers between devices, swap_border(): return lax.ppermute(pieces, 'region', up)  3.89 us
    pallas_call x1, Pallas kernels, shards(): pl.pallas_call(sort_kernel, out_shape=(i32(cells, capacity), i32(1, cells...  2.68 us
    pallas_call x1, Pallas kernels, shards(): pl.pallas_call(pack_kernel, out_shape=(f32(cells, ROWS, capacity), f32(ce...  2.29 us
  transfers between devices with their start and end apart: 4, of which 1 were waited for; matrix products, arithmetic and copies ran while one was open for 0% of the time, Pallas kernels for 21%

commit v1 on v0

--- a/solution.py
+++ b/solution.py
@@ -20,6 +20,11 @@
 X, Y, Z, MASS, VX, VY, VZ, WIDE = range(ROWS)
 HEAT, DENS, LIVE = range(3)
 SENT = 4
+SPEED = 40.0
+ACTIVE, STEP = SENT, SENT + 1
+S_HEAT, S_RANK, S_REACH, S_CHOSEN = range(ROWS, ROWS + 4)
+S_LOW, S_HIGH, S_ROWS = 2 * ROWS, 3 * ROWS, 4 * ROWS
+F_RANK, F_ACTIVE, F_STEP, F_VX, F_VY, F_VZ, F_DENS = range(7)
 INV6, HALF, SOUND, WARM, SUPPORT = range(5)
 
 
@@ -42,11 +47,11 @@
 
 
 def pack_kernel(count, *refs):
-    arrays, (own, own_sent, outgoing, border) = refs[:7], refs[7:11]
-    landed, sem = refs[11:-1], refs[-1]
+    arrays, (own, outgoing, border) = refs[:9], refs[9:12]
+    landed, sem = refs[12:-1], refs[-1]
     for copy in start_copies(arrays, landed, sem):
         copy.wait()
-    export, position, velocity, smoothing, mass, energy, density_old = landed
+    export, position, velocity, smoothing, mass, energy, density_old, active, time_bin = landed
     cells = smoothing.shape[0]
     shape = smoothing.shape
     lane = lanes_of(shape)
@@ -55,39 +60,37 @@
     for cell in range(cells):
         counts = jnp.where(row == cell, count[cell], counts)
     mass_live = jnp.where(lane < counts, mass[...], 0.0)
+    zeros = jnp.zeros(shape, jnp.float32)
     rows = (
         position[0], position[1], position[2], mass_live,
-        40.0 * velocity[0], 40.0 * velocity[1], 40.0 * velocity[2], 2.0 * smoothing[...],
+        SPEED * velocity[0], SPEED * velocity[1], SPEED * velocity[2], 2.0 * smoothing[...],
+        (ADIABATIC - 1.0) * energy[...], density_old[...], counts.astype(jnp.float32), zeros,
+        jnp.where(active[...] > 0, 1.0, 0.0),
+        STEP_MAX * jnp.exp2(-time_bin[...].astype(jnp.float32)), zeros, zeros,
     )
     for field, values in enumerate(rows):
         own[:, field, :] = values
-    own_sent[:, HEAT, :] = (ADIABATIC - 1.0) * energy[...]
-    own_sent[:, DENS, :] = density_old[...]
-    own_sent[:, LIVE, :] = counts.astype(jnp.float32)
-    own_sent[:, SENT - 1, :] = jnp.zeros(shape, jnp.float32)
     per_peer, peers = export.shape
     for peer in range(peers):
         for entry in range(per_peer):
             cell = export[entry, peer]
-            outgoing[peer, entry * ROWS : (entry + 1) * ROWS, :] = own[cell]
+            outgoing[peer, entry * ROWS : (entry + 1) * ROWS, :] = own[cell, 0:ROWS, :]
             start = per_peer * ROWS + entry * SENT
-            outgoing[peer, start : start + SENT, :] = own_sent[cell]
+            outgoing[peer, start : start + SENT, :] = own[cell, ROWS : ROWS + SENT, :]
     for side, cell in enumerate((cells - 1, 0)):
-        border[side, 0:ROWS, :] = own[cell]
-        border[side, ROWS : ROWS + SENT, :] = own_sent[cell]
-
-
-def sort_kernel(*refs):
-    rank_out, actives, columns, heat_sorted, wide_sorted, lowest, highest, reach = refs[3:11]
-    landed, sem = refs[11:14], refs[14]
-    for copy in start_copies(refs[:3], landed, sem):
-        copy.wait()
-    own, own_sent, active = landed
-    shape = active.shape
-    cells = shape[0]
+        border[side] = own[cell, 0 : ROWS + SENT, :]
+
+
+def own_rows(own, field):
+    return own[:, ROWS + field, :]
+
+
+def sort_kernel(own, actives, bundle):
+    cells = own.shape[0]
+    shape = (cells, LANES)
     lane = lanes_of(shape)
-    is_active = active[...] > 0
-    ones = jnp.where(is_active, 1.0, 0.0)
+    ones = own_rows(own, ACTIVE)
+    is_active = ones > 0.5
     for cell in range(cells):
         actives[0, cell] = jnp.sum(ones[cell : cell + 1, :]).astype(jnp.int32)
     square = (LANES, LANES)
@@ -97,7 +100,7 @@
     seen = seen.astype(jnp.int32)
     chosen = lane_gather(seen, jnp.full(shape, LANES - 1, jnp.int32))
     others = lane + 1 - seen
-    rank_out[...] = jnp.where(is_active, seen - 1, chosen + others - 1)
+    rank = jnp.where(is_active, seen - 1, chosen + others - 1)
     first_part = lane < chosen
     wanted = jnp.where(first_part, lane, lane - chosen)
     slot = jnp.zeros(shape, jnp.int32)
@@ -107,26 +110,30 @@
         found = jnp.where(first_part, lane_gather(seen, probe), lane_gather(others, probe))
         slot = jnp.where(found <= wanted, slot + step, slot)
         step //= 2
+    bundle[:, S_HEAT, :] = lane_gather(own_rows(own, HEAT), slot)
+    bundle[:, S_RANK, :] = rank.astype(jnp.float32)
+    bundle[:, S_CHOSEN, :] = chosen.astype(jnp.float32)
+    for spare in range(S_CHOSEN + 1, S_LOW):
+        bundle[:, spare, :] = jnp.zeros(shape, jnp.float32)
+    place = lax.broadcasted_iota(jnp.int32, (ROWS, LANES), 0) <= Z
     for cell in range(cells):
         order = jnp.broadcast_to(slot[cell : cell + 1, :], (ROWS, LANES))
-        tile = lane_gather(own[cell], order)
-        columns[cell] = tile.T
+        tile = lane_gather(own[cell, 0:ROWS, :], order)
+        bundle[cell, 0:ROWS, :] = tile
         target = lane < chosen[cell : cell + 1, :]
         low = jnp.min(jnp.where(target, tile, FAR_AWAY), axis=1, keepdims=True)
         high = jnp.max(jnp.where(target, tile, -FAR_AWAY), axis=1, keepdims=True)
-        place = lax.broadcasted_iota(jnp.int32, shape, 0) <= Z
-        lowest[cell] = jnp.where(place, low, -FAR_AWAY)
-        highest[cell] = jnp.where(place, high, FAR_AWAY)
-        reach[cell : cell + 1, :] = jnp.broadcast_to(high[WIDE : WIDE + 1, :], (1, LANES))
-        wide_sorted[cell : cell + 1, :] = tile[WIDE : WIDE + 1, :]
-        warm = jnp.broadcast_to(own_sent[cell, HEAT : HEAT + 1, :], (ROWS, LANES))
-        heat_sorted[cell : cell + 1, :] = lane_gather(warm, order)[0:1, :]
+        bundle[cell, S_LOW : S_LOW + ROWS, :] = jnp.where(place, low, -FAR_AWAY)
+        bundle[cell, S_HIGH : S_HIGH + ROWS, :] = jnp.where(place, high, FAR_AWAY)
+        bundle[cell, S_REACH : S_REACH + 1, :] = jnp.broadcast_to(high[WIDE : WIDE + 1, :], (1, LANES))
 
 
 def source_tiles(own, incoming, border, per_peer):
-    cells, peers = own[0].shape[0], incoming.shape[0]
-    for cell in range(cells):
-        yield cell, lambda c=cell: own[0][c], lambda c=cell: own[1][c]
+    cells, peers = own.shape[0], incoming.shape[0]
+    for cell in range(cells):
+        yield (
+            cell, lambda c=cell: own[c, 0:ROWS, :], lambda c=cell: own[c, ROWS : ROWS + SENT, :]
+        )
     for peer in range(peers):
         for entry in range(per_peer):
             near, sent = entry * ROWS, per_peer * ROWS + entry * SENT
@@ -196,17 +203,17 @@
             one_chunk(pl.multiple_of(done * ROWS, ROWS), size)
 
 
-def density_kernel(per_peer, *refs):
-    arrays, (density, sorted_density, outgoing, outgoing_border) = refs[:13], refs[13:17]
-    landed, (sem, table, shifts, sums, lines) = refs[17:30], refs[30:]
-    copies = start_copies(arrays, landed, sem)
+def density_kernel(
+    per_peer, pair_source, pair_shift, export, actives,
+    own, incoming, border, bundle,
+    density, densities, outgoing, outgoing_border,
+    table, shifts, columns, sums, lines,
+):
     fill_shifts(shifts)
-    for copy in copies:
-        copy.wait()
-    pair_source, pair_shift, export, actives = landed[:4]
-    own, own_sent, incoming, border, rank, columns, wide_sorted, active, density_old = landed[4:]
+    for cell in range(own.shape[0]):
+        columns[cell] = bundle[cell, 0:ROWS, :].T
     cells, peers = own.shape[0], incoming.shape[0]
-    for place, near, _ in source_tiles((own, own_sent), incoming, border, per_peer):
+    for place, near, _ in source_tiles(own, incoming, border, per_peer):
         table[place] = near()
 
     def one_cell(cell, carry):
@@ -237,11 +244,15 @@
     lax.fori_loop(0, cells, one_cell, 0)
     for cell in range(cells):
         lines[cell : cell + 1, :] = sums[cell].T[0:1, :]
-    inverse = 2.0 / wide_sorted[...]
+    inverse = 2.0 / bundle[:, WIDE, :]
     inverse = inverse * inverse * inverse
     summed = lines[...] * (0.25 / math.pi) * (inverse * inverse)
-    sorted_density[...] = summed
-    density[...] = jnp.where(active[...] > 0, lane_gather(summed, rank[...]), density_old[...])
+    rank = bundle[:, S_RANK, :].astype(jnp.int32)
+    density[...] = jnp.where(
+        own_rows(own, ACTIVE) > 0.5, lane_gather(summed, rank), own_rows(own, DENS)
+    )
+    densities[0] = summed
+    densities[1] = density[...]
     for peer in range(peers):
         for entry in range(per_peer):
             outgoing[peer, entry : entry + 1, :] = density[pl.ds(export[entry, peer], 1), :]
@@ -249,22 +260,17 @@
     outgoing_border[1:2, :] = density[0:1, :]
 
 
-def stream_kernel(per_peer, *refs):
-    arrays, (near_out, far_out, starts, orders, more) = refs[:12], refs[12:17]
-    landed, refs = refs[17:29], refs[29:]
-    sems, near_table, far_table, shifts, inside, totals_row, totals, sem = refs[:8]
-    near_streams, far_streams, out_sems = refs[8:]
-    copies = start_copies(arrays, landed, sems)
+def stream_kernel(
+    per_peer, pair_source, pair_shift, own, incoming, border, bundle, densities,
+    near_streams, far_streams, starts, orders, columns, last,
+    near_table, far_table, shifts, inside, totals_row, totals, sem,
+):
     fill_shifts(shifts)
-    for copy in copies:
-        copy.wait()
-    pair_source, pair_shift, own, own_sent, incoming, border = landed[:6]
-    wide_sorted, heat_sorted, sorted_density, lowest, highest, reach = landed[6:]
     cells, pairs = pair_source.shape
     tile_shape = (ROWS, LANES)
     row = lax.broadcasted_iota(jnp.int32, tile_shape, 0)
     lane = lanes_of(tile_shape).astype(jnp.float32)
-    for place, near, sent in source_tiles((own, own_sent), incoming, border, per_peer):
+    for place, near, sent in source_tiles(own, incoming, border, per_peer):
         tile, other = near(), sent()
         near_table[place] = tile
         wide, heat = tile[WIDE : WIDE + 1, :], other[HEAT : HEAT + 1, :]
@@ -279,8 +285,9 @@
         )
 
     def choose(cell, carry):
-        low, high = lowest[cell], highest[cell]
-        widest = reach[pl.ds(cell, 1), :]
+        low = bundle[cell, S_LOW : S_LOW + ROWS, :]
+        high = bundle[cell, S_HIGH : S_HIGH + ROWS, :]
+        widest = bundle[cell, S_REACH : S_REACH + 1, :]
         kept = []
         for pair in range(pairs):
             source = pair_source[cell, pair]
@@ -291,7 +298,9 @@
             limit = jnp.maximum(support, widest)
             keep = (distance < limit * limit) & (support > 0.0)
             kept.append(jnp.where(keep, 1.0, 0.0))
-        kept += [jnp.zeros((1, LANES), jnp.float32)] * (PAIR_ROWS - pairs)
+        target = lane[0:1, :] < bundle[cell, S_CHOSEN : S_CHOSEN + 1, :]
+        kept.append(jnp.where(target, 1.0, 0.0))
+        kept += [jnp.zeros((1, LANES), jnp.float32)] * (PAIR_ROWS - pairs - 1)
         base = pl.multiple_of(cell * PAIR_ROWS, PAIR_ROWS)
         inside[pl.ds(base, PAIR_ROWS), :] = jnp.concatenate(kept, axis=0)
         return carry
@@ -320,26 +329,25 @@
         slot = jnp.where(found <= wanted, slot + step, slot)
         step //= 2
     orders[...] = slot
-    inverse = 2.0 * pl.reciprocal(wide_sorted[...], approx=True)
+    wide, heat, summed = bundle[:, WIDE, :], bundle[:, S_HEAT, :], densities[0]
+    inverse = 2.0 * pl.reciprocal(wide, approx=True)
     inverse = inverse * inverse * inverse
     fields = (
-        inverse * inverse, 0.025 * wide_sorted[...], jnp.sqrt(ADIABATIC * heat_sorted[...]),
-        4.0 * sorted_density[...], heat_sorted[...] / sorted_density[...],
+        inverse * inverse, 0.025 * wide, jnp.sqrt(ADIABATIC * heat), 4.0 * summed, heat / summed,
     )
     for cell in range(cells):
         tile = jnp.zeros(tile_shape, jnp.float32)
         for which, values in enumerate(fields):
             tile = jnp.where(row == which, values[cell : cell + 1, :], tile)
-        more[cell] = tile.T
+        columns[cell] = jnp.concatenate([bundle[cell, 0:ROWS, :], tile], axis=0).T
+    last[:, F_RANK, :] = bundle[:, S_RANK, :]
+    last[:, F_ACTIVE, :] = own_rows(own, ACTIVE)
+    last[:, F_STEP, :] = own_rows(own, STEP)
+    for from_row, to_row in ((VX, F_VX), (VY, F_VY), (VZ, F_VZ)):
+        last[:, to_row, :] = own[:, from_row, :] * (1.0 / SPEED)
+    last[:, F_DENS, :] = densities[1]
+    last[:, F_DENS + 1, :] = jnp.zeros((cells, LANES), jnp.float32)
     copy.wait()
-
-    def leave(cell):
-        return [
-            pltpu.make_async_copy(stream.at[cell], out.at[cell], sems.at[cell])
-            for stream, out, sems in (
-                (near_streams, near_out, out_sems.at[0]), (far_streams, far_out, out_sems.at[1]),
-            )
-        ]
 
     def one_cell(cell, carry):
         tables = (
@@ -357,45 +365,29 @@
         turned += [turned[-1]] * (PAIR_ROWS - pairs)
         for pair, begin in enumerate(begins):
             starts[cell, pair] = begin
+        place = cell * PAIR_ROWS + pairs
+        starts[cell, pairs + 1] = totals[place >> 7, place & (LANES - 1)]
         fill_streams(
             (near_streams.at[cell], far_streams.at[cell]), tables, pair_source,
             lambda pair: begins[pair], lambda pair: turned[pair], cell,
         )
         base = pl.multiple_of(cell * PAIR_ROWS, PAIR_ROWS)
         orders[pl.ds(base, PAIR_ROWS), :] = jnp.concatenate(turned, axis=0)
-        for copy in leave(cell):
-            copy.start()
         return carry
 
     lax.fori_loop(0, cells, one_cell, 0)
-    for cell in range(cells):
-        for copy in leave(cell):
-            copy.wait()
-
-
-def force_kernel(per_peer, *refs):
-    arrays, streams, (acceleration, kicked) = refs[:13], refs[13:15], refs[15:17]
-    landed, sem, landed_streams, stream_sems = refs[17:30], refs[30], refs[31:33], refs[33:35]
-    table, stream, sums, lines = refs[35:]
-    copies = start_copies(arrays, landed, sem)
-
-    def stream_copies(cell):
-        return [
-            pltpu.make_async_copy(source.at[cell], place.at[cell], sems.at[cell])
-            for source, place, sems in zip(streams, landed_streams, stream_sems)
-        ]
-
-    for cell in range(streams[0].shape[0]):
-        for copy in stream_copies(cell):
-            copy.start()
-    for copy in copies:
-        copy.wait()
-    pair_source, starts, actives, columns, more, orders, own_density = landed[:7]
-    new_density, new_border, rank, active, velocity, time_bin = landed[7:]
-    near_streams, far_streams = landed_streams
-    cells, peers = own_density.shape[0], new_density.shape[0]
-    for cell in range(cells):
-        table[cell, 0:1, :] = own_density[cell : cell + 1, :]
+
+
+def force_kernel(
+    per_peer, pair_source, starts,
+    columns, orders, last, new_density, new_border, near_streams, far_streams,
+    acceleration, kicked,
+    table, stream, sums, lines,
+):
+    cells, peers = last.shape[0], new_density.shape[0]
+    pairs = pair_source.shape[1]
+    for cell in range(cells):
+        table[cell, 0:1, :] = last[cell, F_DENS : F_DENS + 1, :]
     for peer in range(peers):
         for entry in range(per_peer):
             place = cells + peer * per_peer + entry
@@ -410,18 +402,15 @@
             lambda pair: starts[cell, pair],
             lambda pair: orders[pl.ds(cell * PAIR_ROWS + pair, 1), :], cell,
         )
-        for copy in stream_copies(cell):
-            copy.wait()
         rounds = (used + FORCE_UNROLL - 1) // FORCE_UNROLL
 
         def one_chunk(base, groups):
             size = groups * ROWS
             mine = columns[cell, pl.ds(base, size), :]
-            mine_more = more[cell, pl.ds(base, size), :]
             place = [spread(mine, field) for field in (X, Y, Z)]
             speed = [spread(mine, field) for field in (VX, VY, VZ)]
             wide = spread(mine, WIDE)
-            inv6, half_, sound, dens4, press = [spread(mine_more, field) for field in range(5)]
+            inv6, half_, sound, dens4, press = [spread(mine, ROWS + field) for field in range(5)]
 
             def blocks(index, totals):
                 for sub in range(FORCE_UNROLL):
@@ -462,7 +451,7 @@
                     totals[c], axis=1, keepdims=True
                 )
 
-        over_targets(actives[0, cell], one_chunk)
+        over_targets(starts[cell, pairs + 1], one_chunk)
         return carry
 
     lax.fori_loop(0, cells, one_cell, 0)
@@ -470,12 +459,12 @@
         turned = sums[cell].T
         for c in range(3):
             lines[c, cell : cell + 1, :] = turned[c : c + 1, :]
-    step = STEP_MAX * jnp.exp2(-time_bin[...].astype(jnp.float32))
+    rank = last[:, F_RANK, :].astype(jnp.int32)
     for c in range(3):
-        gathered = lane_gather(lines[c] * (0.375 / math.pi), rank[...])
-        value = jnp.where(active[...] > 0, gathered, 0.0)
+        gathered = lane_gather(lines[c] * (0.375 / math.pi), rank)
+        value = jnp.where(last[:, F_ACTIVE, :] > 0.5, gathered, 0.0)
         acceleration[c] = value
-        kicked[c] = velocity[c] + value * step
+        kicked[c] = last[:, F_VX + c, :] + value * last[:, F_STEP, :]
 
 
 def shards(
@@ -491,6 +480,8 @@
     vmem = pl.BlockSpec(memory_space=pltpu.VMEM)
     hbm = pl.BlockSpec(memory_space=pltpu.HBM)
     whole = pltpu.CompilerParams(vmem_limit_bytes=64 * 2**20)
+    params = pltpu.CompilerParams(vmem_limit_bytes=24 * 2**20)
+    cost = pl.CostEstimate(flops=10**9, bytes_accessed=1000, transcendentals=0)
     i32 = lambda *shape: jax.ShapeDtypeStruct(shape, jnp.int32)
     sent_rows = per_peer * (ROWS + SENT)
     turned = export.T
@@ -502,19 +493,21 @@
             + [pltpu.SemaphoreType.DMA((len(arrays),))]
         )
 
-    arrays = (turned, position, velocity, smoothing, particle_mass, energy, density_old)
-    own, own_sent, outgoing, border = pl.pallas_call(
+    arrays = (
+        turned, position, velocity, smoothing, particle_mass, energy, density_old, active, time_bin,
+    )
+    own, outgoing, border = pl.pallas_call(
         pack_kernel,
         out_shape=(
-            f32(cells, ROWS, capacity),
-            f32(cells, SENT, capacity),
+            f32(cells, 2 * ROWS, capacity),
             f32(peers, sent_rows, capacity),
             f32(2, ROWS + SENT, capacity),
         ),
-        in_specs=[smem] + [hbm] * 7,
-        out_specs=(vmem,) * 4,
+        in_specs=[smem] + [hbm] * 9,
+        out_specs=(vmem,) * 3,
         scratch_shapes=landing(1, *arrays),
         compiler_params=whole,
+        cost_estimate=cost,
         name="pack",
     )(cell_count, *arrays)
 
@@ -533,72 +526,56 @@
 
     incoming = exchange(outgoing)
     other = swap_border(border)
-    rank, actives, columns, heat_sorted, wide_sorted, lowest, highest, reach = pl.pallas_call(
+    actives, bundle = pl.pallas_call(
         sort_kernel,
-        out_shape=(
-            i32(cells, capacity),
-            i32(1, cells),
-            f32(cells, capacity, ROWS),
-            f32(cells, capacity),
-            f32(cells, capacity),
-            f32(cells, ROWS, capacity),
-            f32(cells, ROWS, capacity),
-            f32(cells, capacity),
-        ),
-        in_specs=[hbm] * 3,
-        out_specs=(vmem, smem) + (vmem,) * 6,
-        scratch_shapes=landing(0, own, own_sent, active),
-        compiler_params=whole,
+        out_shape=(i32(1, cells), f32(cells, S_ROWS, capacity)),
+        in_specs=[vmem],
+        out_specs=(smem, vmem),
+        compiler_params=params,
+        cost_estimate=cost,
         name="sort",
-    )(own, own_sent, active)
-
-    arrays = (
-        pair_source, pair_shift, turned, actives,
-        own, own_sent, incoming, other, rank, columns, wide_sorted, active, density_old,
-    )
-    density, sorted_density, outgoing_density, border_density = pl.pallas_call(
+    )(own)
+
+    density, densities, outgoing_density, border_density = pl.pallas_call(
         functools.partial(density_kernel, per_peer),
         out_shape=(
             f32(cells, capacity),
-            f32(cells, capacity),
+            f32(2, cells, capacity),
             f32(peers, per_peer, capacity),
             f32(2, capacity),
         ),
-        in_specs=[hbm] * 13,
+        in_specs=[smem] * 4 + [vmem] * 4,
         out_specs=(vmem,) * 4,
-        scratch_shapes=landing(4, *arrays)
-        + [
+        scratch_shapes=[
             pltpu.VMEM((sources, ROWS, capacity), jnp.float32),
             pltpu.VMEM((codes, ROWS, capacity), jnp.float32),
             pltpu.VMEM((cells, capacity, ROWS), jnp.float32),
+            pltpu.VMEM((cells, capacity, ROWS), jnp.float32),
             pltpu.VMEM((cells, capacity), jnp.float32),
         ],
-        compiler_params=whole,
+        compiler_params=params,
+        cost_estimate=cost,
         name="density",
-    )(*arrays)
+    )(pair_source, pair_shift, turned, actives, own, incoming, other, bundle)
 
     new_density = exchange(outgoing_density)
     new_border = swap_border(border_density)
     pairs = pair_source.shape[1]
     blocks = pairs + SPARE
     pair_rows = cells * PAIR_ROWS
-    arrays = (
-        pair_source, pair_shift, own, own_sent, incoming, other, wide_sorted, heat_sorted,
-        sorted_density, lowest, highest, reach,
-    )
-    near_streams, far_streams, starts, orders, more = pl.pallas_call(
+    near_streams, far_streams, starts, orders, columns, last = pl.pallas_call(
         functools.partial(stream_kernel, per_peer),
         out_shape=(
             f32(cells, blocks, ROWS, capacity),
             f32(cells, blocks, ROWS, capacity),
-            i32(cells, pairs + 1),
+            i32(cells, pairs + 2),
             i32(pair_rows, capacity),
-            f32(cells, capacity, ROWS),
+            f32(cells, capacity, 2 * ROWS),
+            f32(cells, ROWS, capacity),
         ),
-        in_specs=[hbm] * 12,
-        out_specs=(hbm, hbm, smem, vmem, vmem),
-        scratch_shapes=landing(2, *arrays)
-        + [
+        in_specs=[smem] * 2 + [vmem] * 5,
+        out_specs=(vmem, vmem, smem, vmem, vmem, vmem),
+        scratch_shapes=[
             pltpu.VMEM((sources, ROWS, capacity), jnp.float32),
             pltpu.VMEM((sources, ROWS, capacity), jnp.float32),
             pltpu.VMEM((codes, ROWS, capacity), jnp.float32),
@@ -606,35 +583,30 @@
             pltpu.VMEM((pair_rows // capacity, capacity), jnp.int32),
             pltpu.SMEM((pair_rows // capacity, capacity), jnp.int32),
             pltpu.SemaphoreType.DMA,
-            pltpu.VMEM((cells, blocks, ROWS, capacity), jnp.float32),
-            pltpu.VMEM((cells, blocks, ROWS, capacity), jnp.float32),
-            pltpu.SemaphoreType.DMA((2, cells)),
         ],
-        compiler_params=whole,
+        compiler_params=params,
+        cost_estimate=cost,
         name="streams",
-    )(*arrays)
-
-    arrays = (
-        pair_source, starts, actives,
-        columns, more, orders, density, new_density, new_border, rank, active, velocity, time_bin,
-    )
+    )(pair_source, pair_shift, own, incoming, other, bundle, densities)
+
     acceleration, kicked = pl.pallas_call(
         functools.partial(force_kernel, per_peer),
         out_shape=(f32(3, cells, capacity), f32(3, cells, capacity)),
-        in_specs=[hbm] * 15,
+        in_specs=[smem] * 2 + [vmem] * 7,
         out_specs=(vmem,) * 2,
-        scratch_shapes=landing(3, *arrays)
-        + [pltpu.VMEM(near_streams.shape, jnp.float32)] * 2
-        + [pltpu.SemaphoreType.DMA((cells,))] * 2
-        + [
+        scratch_shapes=[
             pltpu.VMEM((sources, ROWS, capacity), jnp.float32),
             pltpu.VMEM((blocks, ROWS, capacity), jnp.float32),
             pltpu.VMEM((cells, capacity, ROWS), jnp.float32),
             pltpu.VMEM((3, cells, capacity), jnp.float32),
         ],
-        compiler_params=whole,
+        compiler_params=params,
+        cost_estimate=cost,
         name="force",
-    )(*arrays, near_streams, far_streams)
+    )(
+        pair_source, starts, columns, orders, last, new_density, new_border, near_streams,
+        far_streams,
+    )
     return density, acceleration, kicked
 
 

time: 48.5 us -> 45.6 us (0.940); the launches traced: 48.9 us -> 45.3 us
  Pallas kernels: 28 us -> 25.4 us
  starting transfers between devices: 15.4 us -> 13 us
  local copies, waits for them, and re-layouts: 0 us -> 0.85 us
  waiting for transfers between devices: 4.78 us -> 5.38 us
    ppermute x2, starting transfers between devices: 3.89 us -> 2.11 us  [swap_border(): return lax.ppermute(pieces, 'region', up)]
    pallas_call x2, Pallas kernels: 4.97 us -> 3.47 us  [the longest x1 2.3 us: shards(): pl.pallas_call(pack_kernel, out_shape=(f32(cells, 2 * ROWS, capacity), f3...]
    pallas_call x1, Pallas kernels: 7.38 us -> 5.91 us  [shards(): pl.pallas_call(functools.partial(stream_kernel, per_peer), out_shape=(f32...]
    unnamed x0 -> x10, local copies, waits for them, and re-layouts: none -> 0.85 us
    pallas_call x1, Pallas kernels: 5.87 us -> 6.69 us  [shards(): pl.pallas_call(functools.partial(density_kernel, per_peer), out_shape=(f3...]
    all_to_all x2, starting transfers between devices: 11.5 us -> 10.8 us  [exchange(): lax.all_to_all(pieces, 'cell', split_axis=0, concat_axis=0, tiled=True)]
    pallas_call x1, Pallas kernels: 9.8 us -> 9.31 us  [shards(): pl.pallas_call(functools.partial(force_kernel, per_peer), out_shape=(f32(...]
  transfers between devices with their start and end apart: 4 -> 4, of which waited for: 1 -> 2; matrix products, arithmetic and copies ran while one was open for 0% -> 0% of each run, Pallas kernels for 21% -> 16%
where the time goes in v1:
time: 45.6 us; the launch traced here: 45.3 us
  Pallas kernels  25.4 us (56%)
  starting transfers between devices  13 us (29%)
  waiting for transfers between devices  5.38 us (12%)
  local copies, waits for them, and re-layouts  0.85 us (2%)
  between operations  0.71 us (2%)
    all_to_all x2, starting transfers between devices, exchange(): lax.all_to_all(pieces, 'cell', split_axis=0, concat_axis=0, tiled=True)  10.8 us
    pallas_call x1, Pallas kernels, shards(): pl.pallas_call(functools.partial(force_kernel, per_peer), out_shape=(f32(...  9.31 us
    pallas_call x1, Pallas kernels, shards(): pl.pallas_call(functools.partial(density_kernel, per_peer), out_shape=(f3...  6.69 us
    pallas_call x1, Pallas kernels, shards(): pl.pallas_call(functools.partial(stream_kernel, per_peer), out_shape=(f32...  5.91 us
    all_to_all x2, waiting for transfers between devices, exchange(): lax.all_to_all(pieces, 'cell', split_axis=0, concat_axis=0, tiled=True)  4.98 us
    pallas_call x1, Pallas kernels, shards(): pl.pallas_call(pack_kernel, out_shape=(f32(cells, 2 * ROWS, capacity), f3...  2.3 us
    ppermute x2, starting transfers between devices, swap_border(): return lax.ppermute(pieces, 'region', up)  2.11 us
    pallas_call x1, Pallas kernels, shards(): pl.pallas_call(sort_kernel, out_shape=(i32(1, cells), f32(cells, S_ROWS,...  1.17 us
  transfers between devices with their start and end apart: 4, of which 2 were waited for; matrix products, arithmetic and copies ran while one was open for 0% of the time, Pallas kernels for 16%

profile of v1, /device:TPU:0, one launch (start us, length us, event | category | flops | bytes accessed | tf_op | source)
XLA Modules:
  0.0 45.3 jit_solution(10651047182676602337)
XLA Ops:
  0.6 2.3 %pack.1 = (f32[8,16,128]{2,1,0:T(8,128)}, f32[16,24,128]{2,1,0:T(8,128)}, f32[2,12,128]{2,1,0:T(8,128)}) custom-call(s32[8]{0:T(128)} %count.1, s32[2,16]{1,0:T(2,128)} %bitcast.1, f32[3,8,128]{2,1,0:T(8,128)} %refs_1_.1, f32[3,8,128]{2,1,0:T(8,128)} %refs_2_.1, f32[8,128]{1,0:T(8,128)} %refs_3_.1, f32[8,128]{1,0:T(8,128)} %refs_4_.1, f32[8,128]{1,0:T(8,128)} %refs_5_.1, ...), custom_call_target="tpu_custom_call" | custom-call | flops 1000000000 | bytes 1000 | tf_op jit(solution)/shard_map/pack/pallas_call | solution.py:499
  2.9 7.4 %all-to-all-start = ((f32[16,24,128]{2,1,0:T(8,128)}), f32[16,24,128]{2,1,0:T(8,128)S(1)}, u32[]{:S(2)}, u32[]{:S(2)}) async-start(f32[16,24,128]{2,1,0:T(8,128)} %get-tuple-element.22), calls=%async_computation | async-start | bytes 393216 | tf_op jit(solution)/shard_map/all_to_all | solution.py:515
  10.3 1.6 %collective-permute-start = (f32[2,12,128]{2,1,0:T(8,128)}, f32[2,12,128]{2,1,0:T(8,128)S(1)}, u32[]{:S(2)}, u32[]{:S(2)}) collective-permute-start(f32[2,12,128]{2,1,0:T(8,128)} %get-tuple-element.23), channel_id=1, source_target_pairs={{0,16},{16,0},{1,17},{17,1},{2,18},{18,2},{3,19},{19,3},{4,20},{20... | collective-permute-start | bytes 36872 | tf_op jit(solution)/shard_map/ppermute | solution.py:522
  11.9 0.0 copy-start.3
  11.9 0.8 %copy-done.3 = f32[8,16,128]{2,1,0:T(8,128)S(1)} copy-done((f32[8,16,128]{2,1,0:T(8,128)S(1)}, f32[8,16,128]{2,1,0:T(8,128)}, u32[]{:S(2)}) %copy-start.3) | copy-done | bytes 65560
  12.7 0.0 copy-start
  12.7 0.0 copy-start.1
  12.7 0.0 copy-start.2
  12.7 0.0 copy-start.4
  12.8 1.2 %sort.1 = (s32[1,8]{1,0:T(1,128)S(1)}, f32[8,32,128]{2,1,0:T(8,128)S(1)}) custom-call(f32[8,16,128]{2,1,0:T(8,128)S(1)} %copy-done.3), custom_call_target="tpu_custom_call" | custom-call | flops 1000000000 | bytes 1000 | tf_op jit(solution)/shard_map/sort/pallas_call | solution.py:529
  13.9 0.4 collective-permute-done.border
  14.3 5.0 %all-to-all-done.incoming = f32[16,24,128]{2,1,0:T(8,128)S(1)} async-done(((f32[16,24,128]{2,1,0:T(8,128)}), f32[16,24,128]{2,1,0:T(8,128)S(1)}, u32[]{:S(2)}, u32[]{:S(2)}) %all-to-all-start) | async-done | bytes 196640 | tf_op jit(solution)/shard_map/all_to_all | solution.py:515
  19.3 0.0 copy-done
  19.3 0.0 copy-done.1
  19.3 0.0 copy-done.2
  19.3 0.0 copy-done.4
  19.3 6.7 %density.1 = (f32[8,128]{1,0:T(8,128)}, f32[2,8,128]{2,1,0:T(8,128)S(1)}, f32[16,2,128]{2,1,0:T(2,128)}, f32[2,128]{1,0:T(2,128)S(1)}) custom-call(s32[8,27]{1,0:T(8,128)S(1)} %copy-done.1, s32[8,27]{1,0:T(8,128)S(1)} %copy-done, s32[2,16]{1,0:T(2,128)S(1)} %bitcast.2, s32[1,8]{1,0:T(1,128)S(1)} %get-tuple-element.21.actives, f32[8,16,128]{2,1,0:T(8,128)S(1)} %copy-done.4, ...), custom_call_target="tpu_custom_call" | custom-call | flops 1000000000 | bytes 1000 | tf_op jit(solution)/shard_map/density/pallas_call | solution.py:539
  26.0 3.5 %all-to-all-start.1 = ((f32[16,2,128]{2,1,0:T(2,128)}), f32[16,2,128]{2,1,0:T(2,128)S(1)}, u32[]{:S(2)}, u32[]{:S(2)}) async-start(f32[16,2,128]{2,1,0:T(2,128)} %get-tuple-element.31), calls=%async_computation.1 | async-start | bytes 32768 | tf_op jit(solution)/shard_map/all_to_all | solution.py:515
  29.5 0.5 %collective-permute-start.1 = (f32[2,128]{1,0:T(2,128)S(1)}, f32[2,128]{1,0:T(2,128)S(1)}, u32[]{:S(2)}, u32[]{:S(2)}) collective-permute-start(f32[2,128]{1,0:T(2,128)S(1)} %get-tuple-element.32), channel_id=1, source_target_pairs={{0,16},{16,0},{1,17},{17,1},{2,18},{18,2},{3,19},{19,3},{4,20},{20... | collective-permute-start | bytes 3080 | tf_op jit(solution)/shard_map/ppermute | solution.py:522
  30.0 5.9 %streams.1 = (f32[8,34,8,128]{3,2,1,0:T(8,128)S(1)}, f32[8,34,8,128]{3,2,1,0:T(8,128)S(1)}, s32[8,29]{1,0:T(8,128)S(1)}, s32[256,128]{1,0:T(8,128)S(1)}, f32[8,1...) custom-call(s32[8,27]{1,0:T(8,128)S(1)} %copy-done.1, s32[8,27]{1,0:T(8,128)S(1)} %copy-done, f32[8,16,128]{2,1,0:T(8,128)S(1)} %copy-done.4, ...), custom_call_target="tpu_custom_call" | custom-call | flops 1000000000 | bytes 1000 | tf_op jit(solution)/shard_map/streams/pallas_call | solution.py:566
  36.0 0.0 collective-permute-done.1.new_border
  36.0 0.0 all-to-all-done.1.new_density
  36.0 9.3 %force.1 = (f32[3,8,128]{2,1,0:T(8,128)}, f32[3,8,128]{2,1,0:T(8,128)}) custom-call(s32[8,27]{1,0:T(8,128)S(1)} %copy-done.1, s32[8,29]{1,0:T(8,128)S(1)} %get-tuple-element.27.starts, f32[8,128,16]{2,1,0:T(8,128)S(1)} %get-tuple-element.28.columns, s32[256,128]{1,0:T(8,128)S(1)} %get-tuple-element.29.orders, f32[8,8,128]{2,1,0:T(8,128)S(1)} %get-tuple-element.30.last, ...), custom_call_target="tpu_custom_call" | custom-call | flops 1000000000 | bytes 1000 | tf_op jit(solution)/shard_map/force/pallas_call | solution.py:592
Async XLA Ops:
  2.9 16.4 %all-to-all-start = ((f32[16,24,128]{2,1,0:T(8,128)}), f32[16,24,128]{2,1,0:T(8,128)S(1)}, u32[]{:S(2)}, u32[]{:S(2)}) async-start(f32[16,24,128]{2,1,0:T(8,128)} %get-tuple-element.22), calls=%async_computation | async-start | bytes 393216 | tf_op jit(solution)/shard_map/all_to_all | solution.py:515
  10.3 4.0 %collective-permute-start = (f32[2,12,128]{2,1,0:T(8,128)}, f32[2,12,128]{2,1,0:T(8,128)S(1)}, u32[]{:S(2)}, u32[]{:S(2)}) collective-permute-start(f32[2,12,128]{2,1,0:T(8,128)} %get-tuple-element.23), channel_id=1, source_target_pairs={{0,16},{16,0},{1,17},{17,1},{2,18},{18,2},{3,19},{19,3},{4,20},{20... | collective-permute-start | bytes 36872 | tf_op jit(solution)/shard_map/ppermute | solution.py:522
  11.9 0.8 %copy-start.3 = (f32[8,16,128]{2,1,0:T(8,128)S(1)}, f32[8,16,128]{2,1,0:T(8,128)}, u32[]{:S(2)}) copy-start(f32[8,16,128]{2,1,0:T(8,128)} %get-tuple-element.20.own) | copy-start | bytes 196612
  12.7 6.6 %copy-start = (s32[8,27]{1,0:T(8,128)S(1)}, s32[8,27]{1,0:T(8,128)}, u32[]{:S(2)}) copy-start(s32[8,27]{1,0:T(8,128)} %pair_shift.3) | copy-start | bytes 2596
  12.7 6.6 %copy-start.1 = (s32[8,27]{1,0:T(8,128)S(1)}, s32[8,27]{1,0:T(8,128)}, u32[]{:S(2)}) copy-start(s32[8,27]{1,0:T(8,128)} %pair_source.5) | copy-start | bytes 2596
  12.7 6.6 %copy-start.2 = (s32[16,2]{0,1:T(2,128)S(1)}, s32[16,2]{0,1:T(2,128)}, u32[]{:S(2)}) copy-start(s32[16,2]{0,1:T(2,128)} %param.23) | copy-start | bytes 388
  12.7 6.6 %copy-start.4 = (f32[8,16,128]{2,1,0:T(8,128)S(1)}, f32[8,16,128]{2,1,0:T(8,128)}, u32[]{:S(2)}) copy-start(f32[8,16,128]{2,1,0:T(8,128)} %get-tuple-element.20.own) | copy-start | bytes 196612
  26.0 9.9 %all-to-all-start.1 = ((f32[16,2,128]{2,1,0:T(2,128)}), f32[16,2,128]{2,1,0:T(2,128)S(1)}, u32[]{:S(2)}, u32[]{:S(2)}) async-start(f32[16,2,128]{2,1,0:T(2,128)} %get-tuple-element.31), calls=%async_computation.1 | async-start | bytes 32768 | tf_op jit(solution)/shard_map/all_to_all | solution.py:515
  29.5 6.4 %collective-permute-start.1 = (f32[2,128]{1,0:T(2,128)S(1)}, f32[2,128]{1,0:T(2,128)S(1)}, u32[]{:S(2)}, u32[]{:S(2)}) collective-permute-start(f32[2,128]{1,0:T(2,128)S(1)} %get-tuple-element.32), channel_id=1, source_target_pairs={{0,16},{16,0},{1,17},{17,1},{2,18},{18,2},{3,19},{19,3},{4,20},{20... | collective-permute-start | bytes 3080 | tf_op jit(solution)/shard_map/ppermute | solution.py:522

commit v2 on v1

--- a/solution.py
+++ b/solution.py
@@ -18,6 +18,7 @@
 SPARE = FORCE_UNROLL
 
 X, Y, Z, MASS, VX, VY, VZ, WIDE = range(ROWS)
+SPREAD = (X, Y, Z, WIDE)
 HEAT, DENS, LIVE = range(3)
 SENT = 4
 SPEED = 40.0
@@ -46,12 +47,12 @@
     return copies
 
 
-def pack_kernel(count, *refs):
-    arrays, (own, outgoing, border) = refs[:9], refs[9:12]
-    landed, sem = refs[12:-1], refs[-1]
+def pack_kernel(*refs):
+    arrays, (own, outgoing, border) = refs[:10], refs[10:13]
+    landed, sem = refs[13:-1], refs[-1]
     for copy in start_copies(arrays, landed, sem):
         copy.wait()
-    export, position, velocity, smoothing, mass, energy, density_old, active, time_bin = landed
+    count, export, position, velocity, smoothing, mass, energy, density_old, active, time_bin = landed
     cells = smoothing.shape[0]
     shape = smoothing.shape
     lane = lanes_of(shape)
@@ -85,7 +86,7 @@
     return own[:, ROWS + field, :]
 
 
-def sort_kernel(own, actives, bundle):
+def sort_kernel(own, actives, bundle, spreads, columns):
     cells = own.shape[0]
     shape = (cells, LANES)
     lane = lanes_of(shape)
@@ -126,6 +127,20 @@
         bundle[cell, S_LOW : S_LOW + ROWS, :] = jnp.where(place, low, -FAR_AWAY)
         bundle[cell, S_HIGH : S_HIGH + ROWS, :] = jnp.where(place, high, FAR_AWAY)
         bundle[cell, S_REACH : S_REACH + 1, :] = jnp.broadcast_to(high[WIDE : WIDE + 1, :], (1, LANES))
+        columns[cell] = tile.T
+
+    def one_cell(cell, carry):
+        def one_pair(pair, carry):
+            base = pl.multiple_of(pair * 2 * ROWS, 2 * ROWS)
+            mine = columns[cell, pl.ds(base, 2 * ROWS), :]
+            for which, field in enumerate(SPREAD):
+                tiles = spread(mine, field).reshape(2, ROWS, LANES)
+                spreads[cell, pl.ds(pair * 2, 2), which * ROWS : (which + 1) * ROWS, :] = tiles
+            return carry
+
+        return lax.fori_loop(0, (actives[0, cell] + 2 * ROWS - 1) // (2 * ROWS), one_pair, carry)
+
+    lax.fori_loop(0, cells, one_cell, 0)
 
 
 def source_tiles(own, incoming, border, per_peer):
@@ -180,7 +195,6 @@
         stream[block] = jnp.where(lane < (end & (LANES - 1)), stream[block], 0.0)
         for extra in range(1, SPARE):
             stream[block + extra] = jnp.zeros(shape, jnp.float32)
-    return (end + LANES - 1) >> 7
 
 
 def spread(values, field):
@@ -205,13 +219,11 @@
 
 def density_kernel(
     per_peer, pair_source, pair_shift, export, actives,
-    own, incoming, border, bundle,
+    own, incoming, border, bundle, spreads,
     density, densities, outgoing, outgoing_border,
-    table, shifts, columns, sums, lines,
+    table, shifts, sums, lines,
 ):
     fill_shifts(shifts)
-    for cell in range(own.shape[0]):
-        columns[cell] = bundle[cell, 0:ROWS, :].T
     cells, peers = own.shape[0], incoming.shape[0]
     for place, near, _ in source_tiles(own, incoming, border, per_peer):
         table[place] = near()
@@ -219,9 +231,11 @@
     def one_cell(cell, carry):
         def one_chunk(base, groups):
             size = groups * ROWS
-            mine = columns[cell, pl.ds(base, size), :]
-            place = [spread(mine, field) for field in (X, Y, Z)]
-            wide = spread(mine, WIDE)
+            at = pl.ds(base // ROWS, groups)
+            *place, wide = [
+                spreads[cell, at, which * ROWS : (which + 1) * ROWS, :].reshape(size, LANES)
+                for which in range(len(SPREAD))
+            ]
             smooth = 0.5 * wide
 
             total = jnp.zeros((size, LANES), jnp.float32)
@@ -305,7 +319,7 @@
         inside[pl.ds(base, PAIR_ROWS), :] = jnp.concatenate(kept, axis=0)
         return carry
 
-    lax.fori_loop(0, cells, choose, 0)
+    lax.fori_loop(0, cells, choose, 0, unroll=4)
     flags = inside[...].astype(jnp.bfloat16)
     all_lanes = jnp.ones((ROWS, LANES), jnp.bfloat16)
     sums = lax.dot_general(
@@ -375,14 +389,14 @@
         orders[pl.ds(base, PAIR_ROWS), :] = jnp.concatenate(turned, axis=0)
         return carry
 
-    lax.fori_loop(0, cells, one_cell, 0)
+    lax.fori_loop(0, cells, one_cell, 0, unroll=2)
 
 
 def force_kernel(
     per_peer, pair_source, starts,
     columns, orders, last, new_density, new_border, near_streams, far_streams,
     acceleration, kicked,
-    table, stream, sums, lines,
+    table, streams, sums, lines,
 ):
     cells, peers = last.shape[0], new_density.shape[0]
     pairs = pair_source.shape[1]
@@ -395,13 +409,19 @@
     for side in range(2):
         table[cells + peers * per_peer + side, 0:1, :] = new_border[side : side + 1, :]
 
-    def one_cell(cell, carry):
-        near, far = near_streams.at[cell], far_streams.at[cell]
-        used = fill_streams(
-            (stream,), (lambda source, pair: table[source],), pair_source,
+    def one_stream(cell, carry):
+        fill_streams(
+            (streams.at[cell],), (lambda source, pair: table[source],), pair_source,
             lambda pair: starts[cell, pair],
             lambda pair: orders[pl.ds(cell * PAIR_ROWS + pair, 1), :], cell,
         )
+        return carry
+
+    lax.fori_loop(0, cells, one_stream, 0, unroll=4)
+
+    def one_cell(cell, carry):
+        near, far, stream = near_streams.at[cell], far_streams.at[cell], streams.at[cell]
+        used = (starts[cell, pairs] + LANES - 1) >> 7
         rounds = (used + FORCE_UNROLL - 1) // FORCE_UNROLL
 
         def one_chunk(base, groups):
@@ -494,7 +514,8 @@
         )
 
     arrays = (
-        turned, position, velocity, smoothing, particle_mass, energy, density_old, active, time_bin,
+        cell_count, turned, position, velocity, smoothing, particle_mass, energy, density_old,
+        active, time_bin,
     )
     own, outgoing, border = pl.pallas_call(
         pack_kernel,
@@ -503,13 +524,13 @@
             f32(peers, sent_rows, capacity),
             f32(2, ROWS + SENT, capacity),
         ),
-        in_specs=[smem] + [hbm] * 9,
+        in_specs=[hbm] * 10,
         out_specs=(vmem,) * 3,
-        scratch_shapes=landing(1, *arrays),
+        scratch_shapes=landing(2, *arrays),
         compiler_params=whole,
         cost_estimate=cost,
         name="pack",
-    )(cell_count, *arrays)
+    )(*arrays)
 
     def exchange(pieces):
         return lax.all_to_all(pieces, "cell", split_axis=0, concat_axis=0, tiled=True)
@@ -526,11 +547,16 @@
 
     incoming = exchange(outgoing)
     other = swap_border(border)
-    actives, bundle = pl.pallas_call(
+    actives, bundle, spreads = pl.pallas_call(
         sort_kernel,
-        out_shape=(i32(1, cells), f32(cells, S_ROWS, capacity)),
+        out_shape=(
+            i32(1, cells),
+            f32(cells, S_ROWS, capacity),
+            f32(cells, capacity // ROWS, len(SPREAD) * ROWS, capacity),
+        ),
         in_specs=[vmem],
-        out_specs=(smem, vmem),
+        out_specs=(smem, vmem, vmem),
+        scratch_shapes=[pltpu.VMEM((cells, capacity, ROWS), jnp.float32)],
         compiler_params=params,
         cost_estimate=cost,
         name="sort",
@@ -544,19 +570,18 @@
             f32(peers, per_peer, capacity),
             f32(2, capacity),
         ),
-        in_specs=[smem] * 4 + [vmem] * 4,
+        in_specs=[smem] * 4 + [vmem] * 5,
         out_specs=(vmem,) * 4,
         scratch_shapes=[
             pltpu.VMEM((sources, ROWS, capacity), jnp.float32),
             pltpu.VMEM((codes, ROWS, capacity), jnp.float32),
-            pltpu.VMEM((cells, capacity, ROWS), jnp.float32),
             pltpu.VMEM((cells, capacity, ROWS), jnp.float32),
             pltpu.VMEM((cells, capacity), jnp.float32),
         ],
         compiler_params=params,
         cost_estimate=cost,
         name="density",
-    )(pair_source, pair_shift, turned, actives, own, incoming, other, bundle)
+    )(pair_source, pair_shift, turned, actives, own, incoming, other, bundle, spreads)
 
     new_density = exchange(outgoing_density)
     new_border = swap_border(border_density)
@@ -596,7 +621,7 @@
         out_specs=(vmem,) * 2,
         scratch_shapes=[
             pltpu.VMEM((sources, ROWS, capacity), jnp.float32),
-            pltpu.VMEM((blocks, ROWS, capacity), jnp.float32),
+            pltpu.VMEM((cells, blocks, ROWS, capacity), jnp.float32),
             pltpu.VMEM((cells, capacity, ROWS), jnp.float32),
             pltpu.VMEM((3, cells, capacity), jnp.float32),
         ],

time: 45.6 us -> 42.5 us (0.932)
  the two profiles are of different devices: /device:TPU:0 before, /device:TPU:6 now
where the time goes in v2:
time: 42.5 us; the launch traced here: 42.4 us
  Pallas kernels  25.9 us (61%)
  starting transfers between devices  13.3 us (31%)
  waiting for transfers between devices  1.69 us (4%)
  local copies, waits for them, and re-layouts  0.85 us (2%)
  between operations  0.7 us (2%)
    all_to_all x2, starting transfers between devices, exchange(): lax.all_to_all(pieces, 'cell', split_axis=0, concat_axis=0, tiled=True)  11.6 us
    pallas_call x1, Pallas kernels, shards(): pl.pallas_call(functools.partial(force_kernel, per_peer), out_shape=(f32(...  9.8 us
    pallas_call x1, Pallas kernels, shards(): pl.pallas_call(functools.partial(density_kernel, per_peer), out_shape=(f3...  5.84 us
    pallas_call x1, Pallas kernels, shards(): pl.pallas_call(functools.partial(stream_kernel, per_peer), out_shape=(f32...  5.54 us
    pallas_call x1, Pallas kernels, shards(): pl.pallas_call(sort_kernel, out_shape=(i32(1, cells), f32(cells, S_ROWS,...  3.04 us
    ppermute x2, starting transfers between devices, swap_border(): return lax.ppermute(pieces, 'region', up)  1.73 us
    all_to_all x2, waiting for transfers between devices, exchange(): lax.all_to_all(pieces, 'cell', split_axis=0, concat_axis=0, tiled=True)  1.69 us
    pallas_call x1, Pallas kernels, shards(): pl.pallas_call(pack_kernel, out_shape=(f32(cells, 2 * ROWS, capacity), f3...  1.64 us
  transfers between devices with their start and end apart: 4, of which 1 were waited for; matrix products, arithmetic and copies ran while one was open for 0% of the time, Pallas kernels for 20%

profile of v2, /device:TPU:6, one launch (start us, length us, event | category | flops | bytes accessed | tf_op | source)
XLA Modules:
  0.0 42.4 jit_solution(17650294264275923421)
XLA Ops:
  0.6 1.6 %pack.1 = (f32[8,16,128]{2,1,0:T(8,128)}, f32[16,24,128]{2,1,0:T(8,128)}, f32[2,12,128]{2,1,0:T(8,128)}) custom-call(s32[8]{0:T(128)} %refs_0_.1, s32[2,16]{1,0:T(2,128)} %bitcast.1, f32[3,8,128]{2,1,0:T(8,128)} %refs_2_.1, f32[3,8,128]{2,1,0:T(8,128)} %refs_3_.1, f32[8,128]{1,0:T(8,128)} %refs_4_.1, f32[8,128]{1,0:T(8,128)} %refs_5_.1, f32[8,128]{1,0:T(8,128)} %refs_6_.1, ...), custom_call_target="tpu_custom_call" | custom-call | flops 1000000000 | bytes 1000 | tf_op jit(solution)/shard_map/pack/pallas_call | solution.py:520
  2.3 6.4 %all-to-all-start = ((f32[16,24,128]{2,1,0:T(8,128)}), f32[16,24,128]{2,1,0:T(8,128)S(1)}, u32[]{:S(2)}, u32[]{:S(2)}) async-start(f32[16,24,128]{2,1,0:T(8,128)} %get-tuple-element.23), calls=%async_computation | async-start | bytes 393216 | tf_op jit(solution)/shard_map/all_to_all | solution.py:536
  8.7 0.5 %collective-permute-start = (f32[2,12,128]{2,1,0:T(8,128)}, f32[2,12,128]{2,1,0:T(8,128)S(1)}, u32[]{:S(2)}, u32[]{:S(2)}) collective-permute-start(f32[2,12,128]{2,1,0:T(8,128)} %get-tuple-element.24), channel_id=1, source_target_pairs={{0,16},{16,0},{1,17},{17,1},{2,18},{18,2},{3,19},{19,3},{4,20},{20... | collective-permute-start | bytes 36872 | tf_op jit(solution)/shard_map/ppermute | solution.py:543
  9.2 0.0 copy-start.3
  9.2 0.8 %copy-done.3 = f32[8,16,128]{2,1,0:T(8,128)S(1)} copy-done((f32[8,16,128]{2,1,0:T(8,128)S(1)}, f32[8,16,128]{2,1,0:T(8,128)}, u32[]{:S(2)}) %copy-start.3) | copy-done | bytes 65560
  10.0 0.0 copy-start
  10.0 0.0 copy-start.1
  10.0 0.0 copy-start.2
  10.0 0.0 copy-start.4
  10.0 3.0 %sort.1 = (s32[1,8]{1,0:T(1,128)S(1)}, f32[8,32,128]{2,1,0:T(8,128)S(1)}, f32[8,16,32,128]{3,2,1,0:T(8,128)S(1)}) custom-call(f32[8,16,128]{2,1,0:T(8,128)S(1)} %copy-done.3), custom_call_target="tpu_custom_call" | custom-call | flops 1000000000 | bytes 1000 | tf_op jit(solution)/shard_map/sort/pallas_call | solution.py:550
  13.1 0.0 collective-permute-done.border
  13.1 1.7 %all-to-all-done.incoming = f32[16,24,128]{2,1,0:T(8,128)S(1)} async-done(((f32[16,24,128]{2,1,0:T(8,128)}), f32[16,24,128]{2,1,0:T(8,128)S(1)}, u32[]{:S(2)}, u32[]{:S(2)}) %all-to-all-start) | async-done | bytes 196640 | tf_op jit(solution)/shard_map/all_to_all | solution.py:536
  14.8 0.0 copy-done
  14.8 0.0 copy-done.1
  14.8 0.0 copy-done.2
  14.8 0.0 copy-done.4
  14.8 5.8 %density.1 = (f32[8,128]{1,0:T(8,128)}, f32[2,8,128]{2,1,0:T(8,128)S(1)}, f32[16,2,128]{2,1,0:T(2,128)}, f32[2,128]{1,0:T(2,128)S(1)}) custom-call(s32[8,27]{1,0:T(8,128)S(1)} %copy-done.1, s32[8,27]{1,0:T(8,128)S(1)} %copy-done, s32[2,16]{1,0:T(2,128)S(1)} %bitcast.2, s32[1,8]{1,0:T(1,128)S(1)} %get-tuple-element.22.actives, f32[8,16,128]{2,1,0:T(8,128)S(1)} %copy-done.4, ...), custom_call_target="tpu_custom_call" | custom-call | flops 1000000000 | bytes 1000 | tf_op jit(solution)/shard_map/density/pallas_call | solution.py:565
  20.6 5.2 %all-to-all-start.1 = ((f32[16,2,128]{2,1,0:T(2,128)}), f32[16,2,128]{2,1,0:T(2,128)S(1)}, u32[]{:S(2)}, u32[]{:S(2)}) async-start(f32[16,2,128]{2,1,0:T(2,128)} %get-tuple-element.33), calls=%async_computation.1 | async-start | bytes 32768 | tf_op jit(solution)/shard_map/all_to_all | solution.py:536
  25.8 1.2 %collective-permute-start.1 = (f32[2,128]{1,0:T(2,128)S(1)}, f32[2,128]{1,0:T(2,128)S(1)}, u32[]{:S(2)}, u32[]{:S(2)}) collective-permute-start(f32[2,128]{1,0:T(2,128)S(1)} %get-tuple-element.34), channel_id=1, source_target_pairs={{0,16},{16,0},{1,17},{17,1},{2,18},{18,2},{3,19},{19,3},{4,20},{20... | collective-permute-start | bytes 3080 | tf_op jit(solution)/shard_map/ppermute | solution.py:543
  27.0 5.5 %streams.1 = (f32[8,34,8,128]{3,2,1,0:T(8,128)S(1)}, f32[8,34,8,128]{3,2,1,0:T(8,128)S(1)}, s32[8,29]{1,0:T(8,128)S(1)}, s32[256,128]{1,0:T(8,128)S(1)}, f32[8,1...) custom-call(s32[8,27]{1,0:T(8,128)S(1)} %copy-done.1, s32[8,27]{1,0:T(8,128)S(1)} %copy-done, f32[8,16,128]{2,1,0:T(8,128)S(1)} %copy-done.4, ...), custom_call_target="tpu_custom_call" | custom-call | flops 1000000000 | bytes 1000 | tf_op jit(solution)/shard_map/streams/pallas_call | solution.py:591
  32.6 0.0 collective-permute-done.1.new_border
  32.6 0.0 all-to-all-done.1.new_density
  32.6 9.8 %force.1 = (f32[3,8,128]{2,1,0:T(8,128)}, f32[3,8,128]{2,1,0:T(8,128)}) custom-call(s32[8,27]{1,0:T(8,128)S(1)} %copy-done.1, s32[8,29]{1,0:T(8,128)S(1)} %get-tuple-element.29.starts, f32[8,128,16]{2,1,0:T(8,128)S(1)} %get-tuple-element.30.columns, s32[256,128]{1,0:T(8,128)S(1)} %get-tuple-element.31.orders, f32[8,8,128]{2,1,0:T(8,128)S(1)} %get-tuple-element.32.last, ...), custom_call_target="tpu_custom_call" | custom-call | flops 1000000000 | bytes 1000 | tf_op jit(solution)/shard_map/force/pallas_call | solution.py:617
Async XLA Ops:
  2.3 12.5 %all-to-all-start = ((f32[16,24,128]{2,1,0:T(8,128)}), f32[16,24,128]{2,1,0:T(8,128)S(1)}, u32[]{:S(2)}, u32[]{:S(2)}) async-start(f32[16,24,128]{2,1,0:T(8,128)} %get-tuple-element.23), calls=%async_computation | async-start | bytes 393216 | tf_op jit(solution)/shard_map/all_to_all | solution.py:536
  8.7 4.4 %collective-permute-start = (f32[2,12,128]{2,1,0:T(8,128)}, f32[2,12,128]{2,1,0:T(8,128)S(1)}, u32[]{:S(2)}, u32[]{:S(2)}) collective-permute-start(f32[2,12,128]{2,1,0:T(8,128)} %get-tuple-element.24), channel_id=1, source_target_pairs={{0,16},{16,0},{1,17},{17,1},{2,18},{18,2},{3,19},{19,3},{4,20},{20... | collective-permute-start | bytes 36872 | tf_op jit(solution)/shard_map/ppermute | solution.py:543
  9.2 0.8 %copy-start.3 = (f32[8,16,128]{2,1,0:T(8,128)S(1)}, f32[8,16,128]{2,1,0:T(8,128)}, u32[]{:S(2)}) copy-start(f32[8,16,128]{2,1,0:T(8,128)} %get-tuple-element.21.own) | copy-start | bytes 196612
  10.0 4.8 %copy-start = (s32[8,27]{1,0:T(8,128)S(1)}, s32[8,27]{1,0:T(8,128)}, u32[]{:S(2)}) copy-start(s32[8,27]{1,0:T(8,128)} %pair_shift.3) | copy-start | bytes 2596
  10.0 4.8 %copy-start.1 = (s32[8,27]{1,0:T(8,128)S(1)}, s32[8,27]{1,0:T(8,128)}, u32[]{:S(2)}) copy-start(s32[8,27]{1,0:T(8,128)} %pair_source.5) | copy-start | bytes 2596
  10.0 4.8 %copy-start.2 = (s32[16,2]{0,1:T(2,128)S(1)}, s32[16,2]{0,1:T(2,128)}, u32[]{:S(2)}) copy-start(s32[16,2]{0,1:T(2,128)} %param.23) | copy-start | bytes 388
  10.0 4.8 %copy-start.4 = (f32[8,16,128]{2,1,0:T(8,128)S(1)}, f32[8,16,128]{2,1,0:T(8,128)}, u32[]{:S(2)}) copy-start(f32[8,16,128]{2,1,0:T(8,128)} %get-tuple-element.21.own) | copy-start | bytes 196612
  20.6 12.0 %all-to-all-start.1 = ((f32[16,2,128]{2,1,0:T(2,128)}), f32[16,2,128]{2,1,0:T(2,128)S(1)}, u32[]{:S(2)}, u32[]{:S(2)}) async-start(f32[16,2,128]{2,1,0:T(2,128)} %get-tuple-element.33), calls=%async_computation.1 | async-start | bytes 32768 | tf_op jit(solution)/shard_map/all_to_all | solution.py:536
  25.8 6.8 %collective-permute-start.1 = (f32[2,128]{1,0:T(2,128)S(1)}, f32[2,128]{1,0:T(2,128)S(1)}, u32[]{:S(2)}, u32[]{:S(2)}) collective-permute-start(f32[2,128]{1,0:T(2,128)S(1)} %get-tuple-element.34), channel_id=1, source_target_pairs={{0,16},{16,0},{1,17},{17,1},{2,18},{18,2},{3,19},{19,3},{4,20},{20... | collective-permute-start | bytes 3080 | tf_op jit(solution)/shard_map/ppermute | solution.py:543

commit v3 on v2

--- a/solution.py
+++ b/solution.py
@@ -26,7 +26,8 @@
 S_HEAT, S_RANK, S_REACH, S_CHOSEN = range(ROWS, ROWS + 4)
 S_LOW, S_HIGH, S_ROWS = 2 * ROWS, 3 * ROWS, 4 * ROWS
 F_RANK, F_ACTIVE, F_STEP, F_VX, F_VY, F_VZ, F_DENS = range(7)
-INV6, HALF, SOUND, WARM, SUPPORT = range(5)
+INV6, HALF, SOUND, SUPPORT = range(4)
+DENS4, PRESS = range(2)
 
 
 def lane_gather(values, index):
@@ -245,7 +246,7 @@
                 shift = lambda field: shifts[code, field : field + 1, :]
                 apart = [place[c] - (s(c) + shift(c)) for c in range(3)]
                 square = apart[0] * apart[0] + apart[1] * apart[1] + apart[2] * apart[2]
-                radius = square * lax.rsqrt(jnp.maximum(square, 1e-24))
+                radius = pl.reciprocal(lax.rsqrt(square), approx=True)
                 outer = jnp.maximum(wide - radius, 0.0)
                 inner = jnp.maximum(smooth - radius, 0.0)
                 value = outer * outer * outer - 4.0 * (inner * inner * inner)
@@ -276,7 +277,7 @@
 
 def stream_kernel(
     per_peer, pair_source, pair_shift, own, incoming, border, bundle, densities,
-    near_streams, far_streams, starts, orders, columns, last,
+    near_streams, far_streams, starts, orders, columns, last, heats,
     near_table, far_table, shifts, inside, totals_row, totals, sem,
 ):
     fill_shifts(shifts)
@@ -293,7 +294,7 @@
         far_table[place, INV6 : INV6 + 1, :] = inverse * inverse
         far_table[place, HALF : HALF + 1, :] = 0.025 * wide
         far_table[place, SOUND : SOUND + 1, :] = jnp.sqrt(ADIABATIC * heat)
-        far_table[place, WARM : WARM + 1, :] = heat
+        heats[place : place + 1, :] = heat
         far_table[place, SUPPORT : SUPPORT + 1, :] = jnp.where(
             lane[0:1, :] < other[LIVE : LIVE + 1, :], wide, -FAR_AWAY
         )
@@ -343,12 +344,8 @@
         slot = jnp.where(found <= wanted, slot + step, slot)
         step //= 2
     orders[...] = slot
-    wide, heat, summed = bundle[:, WIDE, :], bundle[:, S_HEAT, :], densities[0]
-    inverse = 2.0 * pl.reciprocal(wide, approx=True)
-    inverse = inverse * inverse * inverse
-    fields = (
-        inverse * inverse, 0.025 * wide, jnp.sqrt(ADIABATIC * heat), 4.0 * summed, heat / summed,
-    )
+    heat, summed = bundle[:, S_HEAT, :], densities[0]
+    fields = (jnp.sqrt(ADIABATIC * heat), 4.0 * summed)
     for cell in range(cells):
         tile = jnp.zeros(tile_shape, jnp.float32)
         for which, values in enumerate(fields):
@@ -394,20 +391,24 @@
 
 def force_kernel(
     per_peer, pair_source, starts,
-    columns, orders, last, new_density, new_border, near_streams, far_streams,
+    columns, orders, last, heats, new_density, new_border, near_streams, far_streams,
     acceleration, kicked,
-    table, streams, sums, lines,
+    table, densities, streams, sums, lines,
 ):
     cells, peers = last.shape[0], new_density.shape[0]
     pairs = pair_source.shape[1]
     for cell in range(cells):
-        table[cell, 0:1, :] = last[cell, F_DENS : F_DENS + 1, :]
+        densities[cell : cell + 1, :] = last[cell, F_DENS : F_DENS + 1, :]
     for peer in range(peers):
-        for entry in range(per_peer):
-            place = cells + peer * per_peer + entry
-            table[place, 0:1, :] = new_density[peer, entry : entry + 1, :]
-    for side in range(2):
-        table[cells + peers * per_peer + side, 0:1, :] = new_border[side : side + 1, :]
+        place = cells + peer * per_peer
+        densities[place : place + per_peer, :] = new_density[peer]
+    place = cells + peers * per_peer
+    densities[place : place + 2, :] = new_border[...]
+    dens4 = 4.0 * densities[...]
+    press = heats[...] * pl.reciprocal(densities[...], approx=True)
+    for place in range(table.shape[0]):
+        table[place, DENS4 : DENS4 + 1, :] = dens4[place : place + 1, :]
+        table[place, PRESS : PRESS + 1, :] = press[place : place + 1, :]
 
     def one_stream(cell, carry):
         fill_streams(
@@ -428,28 +429,31 @@
             size = groups * ROWS
             mine = columns[cell, pl.ds(base, size), :]
             place = [spread(mine, field) for field in (X, Y, Z)]
+            wide = spread(mine, WIDE)
             speed = [spread(mine, field) for field in (VX, VY, VZ)]
-            wide = spread(mine, WIDE)
-            inv6, half_, sound, dens4, press = [spread(mine, ROWS + field) for field in range(5)]
+            sound, dens4 = [spread(mine, ROWS + field) for field in range(2)]
+            inv6 = 2.0 * pl.reciprocal(wide, approx=True)
+            inv6 = inv6 * inv6 * inv6
+            inv6 = inv6 * inv6
+            half_ = 0.025 * wide
+            press = sound * sound * ((4.0 / ADIABATIC) * pl.reciprocal(dens4, approx=True))
 
             def blocks(index, totals):
                 for sub in range(FORCE_UNROLL):
                     block = index * FORCE_UNROLL + sub
                     s = lambda field: near[block, field : field + 1, :]
                     o = lambda field: far[block, field : field + 1, :]
-                    dens = stream[block, 0:1, :]
-                    their_press = o(WARM) * pl.reciprocal(jnp.maximum(dens, 1e-30), approx=True)
+                    m = lambda field: stream[block, field : field + 1, :]
                     apart = [place[c] - s(c) for c in range(3)]
                     square = apart[0] * apart[0] + apart[1] * apart[1] + apart[2] * apart[2]
                     inverse = lax.rsqrt(jnp.maximum(square, 1e-24))
-                    radius = square * inverse
-                    double = radius + radius
+                    radius = pl.reciprocal(inverse, approx=True)
                     outer = jnp.maximum(wide - radius, 0.0)
-                    inner = jnp.maximum(wide - double, 0.0)
-                    slope = inv6 * (outer * outer - inner * inner)
+                    least = jnp.minimum(outer, radius)
+                    slope = inv6 * (least * ((outer + outer) - least))
                     outer = jnp.maximum(s(WIDE) - radius, 0.0)
-                    inner = jnp.maximum(s(WIDE) - double, 0.0)
-                    slope = slope + o(INV6) * (outer * outer - inner * inner)
+                    least = jnp.minimum(outer, radius)
+                    slope = slope + o(INV6) * (least * ((outer + outer) - least))
                     approach = (
                         (speed[0] - s(VX)) * apart[0]
                         + (speed[1] - s(VY)) * apart[1]
@@ -458,14 +462,14 @@
                     half = half_ + o(HALF)
                     slow = pl.reciprocal(square + half * half, approx=True)
                     mu = half * jnp.minimum(approach, 0.0) * slow
-                    light = pl.reciprocal(dens4 + 4.0 * dens, approx=True)
+                    light = pl.reciprocal(dens4 + m(DENS4), approx=True)
                     viscous = mu * (mu - (sound + o(SOUND))) * light
-                    weight = (press + their_press + viscous) * (slope * (inverse * s(MASS)))
-                    totals = tuple(total + weight * a for total, a in zip(totals, apart))
-                return totals
-
-            zero = jnp.zeros((size, LANES), jnp.float32)
-            totals = lax.fori_loop(0, rounds, blocks, (zero, zero, zero))
+                    weight = (press + m(PRESS) + viscous) * (slope * (inverse * s(MASS)))
+                    terms = [weight * a for a in apart]
+                    totals = terms if totals is None else [t + a for t, a in zip(totals, terms)]
+                return tuple(totals)
+
+            totals = lax.fori_loop(1, rounds, blocks, blocks(0, None))
             for c in range(3):
                 sums[cell, pl.ds(base, size), c : c + 1] = jnp.sum(
                     totals[c], axis=1, keepdims=True
@@ -588,7 +592,8 @@
     pairs = pair_source.shape[1]
     blocks = pairs + SPARE
     pair_rows = cells * PAIR_ROWS
-    near_streams, far_streams, starts, orders, columns, last = pl.pallas_call(
+    source_rows = -(-sources // ROWS) * ROWS
+    near_streams, far_streams, starts, orders, columns, last, heats = pl.pallas_call(
         functools.partial(stream_kernel, per_peer),
         out_shape=(
             f32(cells, blocks, ROWS, capacity),
@@ -597,9 +602,10 @@
             i32(pair_rows, capacity),
             f32(cells, capacity, 2 * ROWS),
             f32(cells, ROWS, capacity),
+            f32(source_rows, capacity),
         ),
         in_specs=[smem] * 2 + [vmem] * 5,
-        out_specs=(vmem, vmem, smem, vmem, vmem, vmem),
+        out_specs=(vmem, vmem, smem, vmem, vmem, vmem, vmem),
         scratch_shapes=[
             pltpu.VMEM((sources, ROWS, capacity), jnp.float32),
             pltpu.VMEM((sources, ROWS, capacity), jnp.float32),
@@ -617,10 +623,11 @@
     acceleration, kicked = pl.pallas_call(
         functools.partial(force_kernel, per_peer),
         out_shape=(f32(3, cells, capacity), f32(3, cells, capacity)),
-        in_specs=[smem] * 2 + [vmem] * 7,
+        in_specs=[smem] * 2 + [vmem] * 8,
         out_specs=(vmem,) * 2,
         scratch_shapes=[
             pltpu.VMEM((sources, ROWS, capacity), jnp.float32),
+            pltpu.VMEM((source_rows, capacity), jnp.float32),
             pltpu.VMEM((cells, blocks, ROWS, capacity), jnp.float32),
             pltpu.VMEM((cells, capacity, ROWS), jnp.float32),
             pltpu.VMEM((3, cells, capacity), jnp.float32),
@@ -629,7 +636,7 @@
         cost_estimate=cost,
         name="force",
     )(
-        pair_source, starts, columns, orders, last, new_density, new_border, near_streams,
+        pair_source, starts, columns, orders, last, heats, new_density, new_border, near_streams,
         far_streams,
     )
     return density, acceleration, kicked

time: 42.5 us -> 43.4 us (1.021)
  the two profiles are of different devices: /device:TPU:6 before, /device:TPU:1 now
where the time goes in v3:
time: 43.4 us; the launch traced here: 43.5 us
  Pallas kernels  25.3 us (58%)
  starting transfers between devices  13.4 us (31%)
  waiting for transfers between devices  3.18 us (7%)
  local copies, waits for them, and re-layouts  0.85 us (2%)
  between operations  0.71 us (2%)
    all_to_all x2, starting transfers between devices, exchange(): lax.all_to_all(pieces, 'cell', split_axis=0, concat_axis=0, tiled=True)  10.7 us
    pallas_call x1, Pallas kernels, shards(): pl.pallas_call(functools.partial(force_kernel, per_peer), out_shape=(f32(...  9.51 us
    pallas_call x1, Pallas kernels, shards(): pl.pallas_call(functools.partial(density_kernel, per_peer), out_shape=(f3...  5.61 us
    pallas_call x1, Pallas kernels, shards(): pl.pallas_call(functools.partial(stream_kernel, per_peer), out_shape=(f32...  5.52 us
    all_to_all x2, waiting for transfers between devices, exchange(): lax.all_to_all(pieces, 'cell', split_axis=0, concat_axis=0, tiled=True)  3.17 us
    pallas_call x1, Pallas kernels, shards(): pl.pallas_call(sort_kernel, out_shape=(i32(1, cells), f32(cells, S_ROWS,...  3.04 us
    ppermute x2, starting transfers between devices, swap_border(): return lax.ppermute(pieces, 'region', up)  2.75 us
    pallas_call x1, Pallas kernels, shards(): pl.pallas_call(pack_kernel, out_shape=(f32(cells, 2 * ROWS, capacity), f3...  1.64 us
  transfers between devices with their start and end apart: 4, of which 1 were waited for; matrix products, arithmetic and copies ran while one was open for 0% of the time, Pallas kernels for 20%

profile of v3, /device:TPU:1, one launch (start us, length us, event | category | flops | bytes accessed | tf_op | source)
XLA Modules:
  0.0 43.5 jit_solution(11571677845032168532)
XLA Ops:
  0.6 1.6 %pack.1 = (f32[8,16,128]{2,1,0:T(8,128)}, f32[16,24,128]{2,1,0:T(8,128)}, f32[2,12,128]{2,1,0:T(8,128)}) custom-call(s32[8]{0:T(128)} %refs_0_.1, s32[2,16]{1,0:T(2,128)} %bitcast.1, f32[3,8,128]{2,1,0:T(8,128)} %refs_2_.1, f32[3,8,128]{2,1,0:T(8,128)} %refs_3_.1, f32[8,128]{1,0:T(8,128)} %refs_4_.1, f32[8,128]{1,0:T(8,128)} %refs_5_.1, f32[8,128]{1,0:T(8,128)} %refs_6_.1, ...), custom_call_target="tpu_custom_call" | custom-call | flops 1000000000 | bytes 1000 | tf_op jit(solution)/shard_map/pack/pallas_call | solution.py:524
  2.3 7.3 %all-to-all-start = ((f32[16,24,128]{2,1,0:T(8,128)}), f32[16,24,128]{2,1,0:T(8,128)S(1)}, u32[]{:S(2)}, u32[]{:S(2)}) async-start(f32[16,24,128]{2,1,0:T(8,128)} %get-tuple-element.24), calls=%async_computation | async-start | bytes 393216 | tf_op jit(solution)/shard_map/all_to_all | solution.py:540
  9.6 1.2 %collective-permute-start = (f32[2,12,128]{2,1,0:T(8,128)}, f32[2,12,128]{2,1,0:T(8,128)S(1)}, u32[]{:S(2)}, u32[]{:S(2)}) collective-permute-start(f32[2,12,128]{2,1,0:T(8,128)} %get-tuple-element.25), channel_id=1, source_target_pairs={{0,16},{16,0},{1,17},{17,1},{2,18},{18,2},{3,19},{19,3},{4,20},{20... | collective-permute-start | bytes 36872 | tf_op jit(solution)/shard_map/ppermute | solution.py:547
  10.9 0.0 copy-start.3
  10.9 0.8 %copy-done.3 = f32[8,16,128]{2,1,0:T(8,128)S(1)} copy-done((f32[8,16,128]{2,1,0:T(8,128)S(1)}, f32[8,16,128]{2,1,0:T(8,128)}, u32[]{:S(2)}) %copy-start.3) | copy-done | bytes 65560
  11.7 0.0 copy-start
  11.7 0.0 copy-start.1
  11.7 0.0 copy-start.2
  11.7 0.0 copy-start.4
  11.7 3.0 %sort.1 = (s32[1,8]{1,0:T(1,128)S(1)}, f32[8,32,128]{2,1,0:T(8,128)S(1)}, f32[8,16,32,128]{3,2,1,0:T(8,128)S(1)}) custom-call(f32[8,16,128]{2,1,0:T(8,128)S(1)} %copy-done.3), custom_call_target="tpu_custom_call" | custom-call | flops 1000000000 | bytes 1000 | tf_op jit(solution)/shard_map/sort/pallas_call | solution.py:554
  14.8 0.0 collective-permute-done.border
  14.8 3.2 %all-to-all-done.incoming = f32[16,24,128]{2,1,0:T(8,128)S(1)} async-done(((f32[16,24,128]{2,1,0:T(8,128)}), f32[16,24,128]{2,1,0:T(8,128)S(1)}, u32[]{:S(2)}, u32[]{:S(2)}) %all-to-all-start) | async-done | bytes 196640 | tf_op jit(solution)/shard_map/all_to_all | solution.py:540
  17.9 0.0 copy-done
  17.9 0.0 copy-done.1
  17.9 0.0 copy-done.2
  18.0 0.0 copy-done.4
  18.0 5.6 %density.1 = (f32[8,128]{1,0:T(8,128)}, f32[2,8,128]{2,1,0:T(8,128)S(1)}, f32[16,2,128]{2,1,0:T(2,128)}, f32[2,128]{1,0:T(2,128)S(1)}) custom-call(s32[8,27]{1,0:T(8,128)S(1)} %copy-done.1, s32[8,27]{1,0:T(8,128)S(1)} %copy-done, s32[2,16]{1,0:T(2,128)S(1)} %bitcast.2, s32[1,8]{1,0:T(1,128)S(1)} %get-tuple-element.23.actives, f32[8,16,128]{2,1,0:T(8,128)S(1)} %copy-done.4, ...), custom_call_target="tpu_custom_call" | custom-call | flops 1000000000 | bytes 1000 | tf_op jit(solution)/shard_map/density/pallas_call | solution.py:569
  23.6 3.3 %all-to-all-start.1 = ((f32[16,2,128]{2,1,0:T(2,128)}), f32[16,2,128]{2,1,0:T(2,128)S(1)}, u32[]{:S(2)}, u32[]{:S(2)}) async-start(f32[16,2,128]{2,1,0:T(2,128)} %get-tuple-element.35), calls=%async_computation.1 | async-start | bytes 32768 | tf_op jit(solution)/shard_map/all_to_all | solution.py:540
  26.9 1.5 %collective-permute-start.1 = (f32[2,128]{1,0:T(2,128)S(1)}, f32[2,128]{1,0:T(2,128)S(1)}, u32[]{:S(2)}, u32[]{:S(2)}) collective-permute-start(f32[2,128]{1,0:T(2,128)S(1)} %get-tuple-element.36), channel_id=1, source_target_pairs={{0,16},{16,0},{1,17},{17,1},{2,18},{18,2},{3,19},{19,3},{4,20},{20... | collective-permute-start | bytes 3080 | tf_op jit(solution)/shard_map/ppermute | solution.py:547
  28.4 5.5 %streams.1 = (f32[8,34,8,128]{3,2,1,0:T(8,128)S(1)}, f32[8,34,8,128]{3,2,1,0:T(8,128)S(1)}, s32[8,29]{1,0:T(8,128)S(1)}, s32[256,128]{1,0:T(8,128)S(1)}, f32[8,1...) custom-call(s32[8,27]{1,0:T(8,128)S(1)} %copy-done.1, s32[8,27]{1,0:T(8,128)S(1)} %copy-done, ...), custom_call_target="tpu_custom_call" | custom-call | flops 1000000000 | bytes 1000 | tf_op jit(solution)/shard_map/streams/pallas_call | solution.py:596
  34.0 0.0 collective-permute-done.1.new_border
  34.0 0.0 all-to-all-done.1.new_density
  34.0 9.5 %force.1 = (f32[3,8,128]{2,1,0:T(8,128)}, f32[3,8,128]{2,1,0:T(8,128)}) custom-call(s32[8,27]{1,0:T(8,128)S(1)} %copy-done.1, s32[8,29]{1,0:T(8,128)S(1)} %get-tuple-element.30.starts, f32[8,128,16]{2,1,0:T(8,128)S(1)} %get-tuple-element.31.columns, s32[256,128]{1,0:T(8,128)S(1)} %get-tuple-element.32.orders, f32[8,8,128]{2,1,0:T(8,128)S(1)} %get-tuple-element.33.last, ...), custom_call_target="tpu_custom_call" | custom-call | flops 1000000000 | bytes 1000 | tf_op jit(solution)/shard_map/force/pallas_call | solution.py:623
Async XLA Ops:
  2.3 15.7 %all-to-all-start = ((f32[16,24,128]{2,1,0:T(8,128)}), f32[16,24,128]{2,1,0:T(8,128)S(1)}, u32[]{:S(2)}, u32[]{:S(2)}) async-start(f32[16,24,128]{2,1,0:T(8,128)} %get-tuple-element.24), calls=%async_computation | async-start | bytes 393216 | tf_op jit(solution)/shard_map/all_to_all | solution.py:540
  9.6 5.1 %collective-permute-start = (f32[2,12,128]{2,1,0:T(8,128)}, f32[2,12,128]{2,1,0:T(8,128)S(1)}, u32[]{:S(2)}, u32[]{:S(2)}) collective-permute-start(f32[2,12,128]{2,1,0:T(8,128)} %get-tuple-element.25), channel_id=1, source_target_pairs={{0,16},{16,0},{1,17},{17,1},{2,18},{18,2},{3,19},{19,3},{4,20},{20... | collective-permute-start | bytes 36872 | tf_op jit(solution)/shard_map/ppermute | solution.py:547
  10.9 0.8 %copy-start.3 = (f32[8,16,128]{2,1,0:T(8,128)S(1)}, f32[8,16,128]{2,1,0:T(8,128)}, u32[]{:S(2)}) copy-start(f32[8,16,128]{2,1,0:T(8,128)} %get-tuple-element.22.own) | copy-start | bytes 196612
  11.7 6.2 %copy-start = (s32[8,27]{1,0:T(8,128)S(1)}, s32[8,27]{1,0:T(8,128)}, u32[]{:S(2)}) copy-start(s32[8,27]{1,0:T(8,128)} %pair_shift.3) | copy-start | bytes 2596
  11.7 6.2 %copy-start.1 = (s32[8,27]{1,0:T(8,128)S(1)}, s32[8,27]{1,0:T(8,128)}, u32[]{:S(2)}) copy-start(s32[8,27]{1,0:T(8,128)} %pair_source.5) | copy-start | bytes 2596
  11.7 6.2 %copy-start.2 = (s32[16,2]{0,1:T(2,128)S(1)}, s32[16,2]{0,1:T(2,128)}, u32[]{:S(2)}) copy-start(s32[16,2]{0,1:T(2,128)} %param.23) | copy-start | bytes 388
  11.7 6.2 %copy-start.4 = (f32[8,16,128]{2,1,0:T(8,128)S(1)}, f32[8,16,128]{2,1,0:T(8,128)}, u32[]{:S(2)}) copy-start(f32[8,16,128]{2,1,0:T(8,128)} %get-tuple-element.22.own) | copy-start | bytes 196612
  23.6 10.4 %all-to-all-start.1 = ((f32[16,2,128]{2,1,0:T(2,128)}), f32[16,2,128]{2,1,0:T(2,128)S(1)}, u32[]{:S(2)}, u32[]{:S(2)}) async-start(f32[16,2,128]{2,1,0:T(2,128)} %get-tuple-element.35), calls=%async_computation.1 | async-start | bytes 32768 | tf_op jit(solution)/shard_map/all_to_all | solution.py:540
  26.9 7.0 %collective-permute-start.1 = (f32[2,128]{1,0:T(2,128)S(1)}, f32[2,128]{1,0:T(2,128)S(1)}, u32[]{:S(2)}, u32[]{:S(2)}) collective-permute-start(f32[2,128]{1,0:T(2,128)S(1)} %get-tuple-element.36), channel_id=1, source_target_pairs={{0,16},{16,0},{1,17},{17,1},{2,18},{18,2},{3,19},{19,3},{4,20},{20... | collective-permute-start | bytes 3080 | tf_op jit(solution)/shard_map/ppermute | solution.py:547
